TPU v7x, 128 devices: a whole 4x4x4 slice. The times are simulated.
128 devices in a mesh: row: 8 (over y_hi, z), col: 16 (over y_lo, x, core).
Axes of the slice: x: 4, y: 4 (y_hi: 2, y_lo: 2; y = y_hi * 2 + y_lo), z: 4, core: 2. Of those that a mesh axis runs over, the one named last changes fastest.
Arguments:
- features: bfloat16 [65536, 256], P(('row', 'col')), may hold values from -6 to 6
- weight: bfloat16 [256, 256], replicated, may hold values from -0.375 to 0.375
- bias_term: float32 [256], replicated, may hold values from -3 to 3
- upstream: bfloat16 [65536, 256], P(('row', 'col')), may hold values from -6 to 6
- block_values: bfloat16 [8, 6144, 128, 128], P('row', 'col'), may hold values from -0.07470703 to 0.07470703
- block_rows: int32 [8, 6144], P('row', 'col'), may hold values from 0 to 63
- block_cols: int32 [8, 6144], P('row', 'col'), may hold values from 0 to 31
- live_count: int32 [8, 16], P('row', 'col'), may hold values from 96 to 384, as said below
Outputs:
- activation: bfloat16 [65536, 256], P(('row', 'col'))
- feature_grad: bfloat16 [65536, 256], P(('row', 'col'))
- weight_grad: float32 [256, 256], replicated
- bias_grad: float32 [256], replicated
Inputs may be any that keep to these rules, and one draw needn't show every extreme that they name: `live_count`: every device uses at least a quarter of its slots, and some device uses all 384.
All inputs are finite; a program needn't handle non-finite values.
Results may differ from a plain program's by a relative error of at most 0.007.
Values may be sent and summed in bfloat16 or wider, within the bound.
No kernel may reach another device: no remote copies, remote signals or barrier semaphores. Data moves between devices by JAX's collectives and lax.ppermute only.
A program may use at most 192 MiB of HBM per device.

v0:
```python
import jax
import jax.numpy as jnp
from jax import lax
from jax.sharding import PartitionSpec as P


def block_product(block_vals, source_ids, target_ids, live_mask, source, target_blocks, flipped):
    count_blocks = block_vals.shape[0]
    block_edge = block_vals.shape[1]
    feature_width = source.shape[1]
    group_size = 64
    group_count = count_blocks // group_size
    source_flat = source.reshape(-1, block_edge * feature_width)
    source_count = source_flat.shape[0]
    source_range = jnp.arange(source_count, dtype=jnp.int32)
    target_range = jnp.arange(target_blocks, dtype=jnp.int32)
    einsum_form = "kji,kjf->kif" if flipped else "kij,kjf->kif"

    def group_step(running, group):
        group_vals, group_sources, group_targets, group_live = group
        pick_table = (group_sources[:, None] == source_range[None, :]).astype(jnp.bfloat16)
        pieces = jnp.dot(pick_table, source_flat, preferred_element_type=jnp.float32).astype(
            jnp.bfloat16
        )
        pieces = pieces.reshape(group_size, block_edge, feature_width)
        product = jnp.einsum(einsum_form, group_vals, pieces, preferred_element_type=jnp.float32)
        place_table = (target_range[:, None] == group_targets[None, :]).astype(jnp.float32)
        place_table = place_table * group_live.astype(jnp.float32)[None, :]
        added = jnp.dot(
            place_table,
            product.reshape(group_size, block_edge * feature_width),
            precision=lax.Precision.HIGHEST,
            preferred_element_type=jnp.float32,
        )
        return (running + added, None)

    initial = jnp.zeros((target_blocks, block_edge * feature_width), jnp.float32)
    grouped = (
        block_vals.reshape(group_count, group_size, block_edge, block_edge),
        source_ids.reshape(group_count, group_size),
        target_ids.reshape(group_count, group_size),
        live_mask.reshape(group_count, group_size),
    )
    summed, unused = lax.scan(group_step, initial, grouped)
    return summed.reshape(target_blocks * block_edge, feature_width)


def dense_step(aggregated, weight, bias_term, upstream):
    preact = jnp.dot(aggregated, weight, preferred_element_type=jnp.float32) + bias_term
    sigmoid_val = jax.nn.sigmoid(preact)
    activation = (preact * sigmoid_val).astype(jnp.bfloat16)
    grad_pre = (
        upstream.astype(jnp.float32) * sigmoid_val * (1.0 + preact * (1.0 - sigmoid_val))
    ).astype(jnp.bfloat16)
    grad_mid = jnp.dot(grad_pre, weight.T, preferred_element_type=jnp.float32).astype(jnp.bfloat16)
    return (activation, grad_pre, grad_mid)


def per_device(
    features, weight, bias_term, upstream, block_values, block_rows, block_cols, live_count
):
    node_rows = features.shape[0]
    block_edge = block_values.shape[2]
    block_vals = block_values.reshape(-1, block_edge, block_edge)
    row_ids = block_rows.reshape(-1)
    col_ids = block_cols.reshape(-1)
    slot_ids = jnp.arange(row_ids.shape[0], dtype=jnp.int32)
    live_mask = slot_ids < live_count[0, 0]
    group_blocks = lax.axis_size("col") * node_rows // block_edge
    panel_blocks = lax.axis_size("row") * node_rows // block_edge
    panel = lax.all_gather(features, "row", axis=0, tiled=True)
    partial_value = block_product(
        block_vals, col_ids, row_ids, live_mask, panel, group_blocks, False
    )
    aggregated = lax.psum_scatter(partial_value, "col", scatter_dimension=0, tiled=True).astype(
        jnp.bfloat16
    )
    activation, grad_pre, grad_mid = dense_step(aggregated, weight, bias_term, upstream)
    group_grad = lax.all_gather(grad_mid, "col", axis=0, tiled=True)
    own_aggregated, own_grad = (aggregated, grad_pre)
    weight_term = jnp.dot(own_aggregated.T, own_grad, preferred_element_type=jnp.float32)
    bias_sum = jnp.sum(own_grad.astype(jnp.float32), axis=0)
    weight_total, bias_total = lax.psum((weight_term, bias_sum), ("row", "col"))
    norm_factor = 1.0 / jnp.sqrt(
        jnp.float32(node_rows * lax.axis_size("row") * lax.axis_size("col"))
    )
    panel_partial = block_product(
        block_vals, row_ids, col_ids, live_mask, group_grad, panel_blocks, True
    )
    feature_grad = lax.psum_scatter(panel_partial, "row", scatter_dimension=0, tiled=True).astype(
        jnp.bfloat16
    )
    return (activation, feature_grad, weight_total * norm_factor, bias_total * norm_factor)


def solution(mesh):
    in_specs = (
        P(("row", "col"), None),
        P(),
        P(),
        P(("row", "col"), None),
        P("row", "col", None, None),
        P("row", "col"),
        P("row", "col"),
        P("row", "col"),
    )
    out_specs = (P(("row", "col"), None), P(("row", "col"), None), P(), P())
    return jax.shard_map(
        per_device, mesh=mesh, in_specs=in_specs, out_specs=out_specs, check_vma=False
    )
```

profile of v0, /device:TPU:0, one launch (start us, length us, event | category | flops | bytes accessed | tf_op | source)
XLA Modules:
  0.0 597.4 jit_solution(7979915506011484660)
XLA Ops:
  10.2 56.8 %all-gather.3.cloned.1.call-done = bf16[4096,256]{1,0:T(8,128)(2,1)} async-done(((bf16[512,256]{1,0:T(8,128)(2,1)}), bf16[4096,256]{1,0:T(8,128)(2,1)}) %all-gather.3.cloned.1.call-update) | async-done | bytes 2097168 | tf_op jit(solution)/shard_map/all_gather | solution.py:71
  67.0 2.9 reshape.44
  69.9 157.5 %while.22 = (s32[]{:T(128)}, f32[64,32768]{1,0:T(8,128)}, s32[6,64]{1,0:T(8,128)S(1)}, pred[6,64]{1,0:T(8,128)(4,1)S(1)}, bf16[6,64,128,128]{3,2,1,0:T(8,128)(2,...) while((s32[]{:T(128)}, f32[64,32768]{1,0:T(8,128)}, ...), condition=%wide.region_1.2_spmd.clone, body=%wide.region_0.1_spmd.clone.sunk | while | flops 2288003072 | bytes 71305904 | solution.py:44
  70.0 1.3 convolution_convert_fusion.5
  71.2 1.1 copy.23
  72.3 2.9 fusion.69
  75.2 8.0 %copy.24 = f32[8,8,128,256]{3,1,2,0:T(8,128)} copy(f32[8,8,128,256]{3,2,1,0:T(8,128)S(1)} %bitcast.81) | data formatting | bytes 16777216 | tf_op jit(solution)/shard_map/while
  83.2 12.0 %convolution_add_fusion.5 = f32[64,32768]{1,0:T(8,128)} fusion(f32[64,32768]{1,0:T(8,128)} %bitcast.83, f32[64,32768]{1,0:T(8,128)} %get-tuple-element.302, pred[]{:T(512)S(6)} %compare.6, f32[64]{0:T(128)S(1)} %fusion.70, s32[64]{0:T(128)S(1)} %get-tuple-element.282), kind=kOutput, calls=%fused_computation.4.clone.1 | convolution fusion | flops 1614815232 | bytes 25166336 | tf_op jit(solution)/shard_map/while/body/eval_jaxpr/dot_general | solution.py:29
  95.1 1.3 convolution_convert_fusion.5
  97.5 2.9 fusion.69
  100.4 8.0 %copy.24 = f32[8,8,128,256]{3,1,2,0:T(8,128)} copy(f32[8,8,128,256]{3,2,1,0:T(8,128)S(1)} %bitcast.81) | data formatting | bytes 16777216 | tf_op jit(solution)/shard_map/while
  108.3 13.2 %convolution_add_fusion.5 = f32[64,32768]{1,0:T(8,128)} fusion(f32[64,32768]{1,0:T(8,128)} %bitcast.83, f32[64,32768]{1,0:T(8,128)} %get-tuple-element.302, pred[]{:T(512)S(6)} %compare.6, f32[64]{0:T(128)S(1)} %fusion.70, s32[64]{0:T(128)S(1)} %get-tuple-element.282), kind=kOutput, calls=%fused_computation.4.clone.1 | convolution fusion | flops 1614815232 | bytes 25166336 | tf_op jit(solution)/shard_map/while/body/eval_jaxpr/dot_general | solution.py:29
  121.6 1.3 convolution_convert_fusion.5
  124.0 2.9 fusion.69
  126.9 8.0 %copy.24 = f32[8,8,128,256]{3,1,2,0:T(8,128)} copy(f32[8,8,128,256]{3,2,1,0:T(8,128)S(1)} %bitcast.81) | data formatting | bytes 16777216 | tf_op jit(solution)/shard_map/while
  134.8 13.2 %convolution_add_fusion.5 = f32[64,32768]{1,0:T(8,128)} fusion(f32[64,32768]{1,0:T(8,128)} %bitcast.83, f32[64,32768]{1,0:T(8,128)} %get-tuple-element.302, pred[]{:T(512)S(6)} %compare.6, f32[64]{0:T(128)S(1)} %fusion.70, s32[64]{0:T(128)S(1)} %get-tuple-element.282), kind=kOutput, calls=%fused_computation.4.clone.1 | convolution fusion | flops 1614815232 | bytes 25166336 | tf_op jit(solution)/shard_map/while/body/eval_jaxpr/dot_general | solution.py:29
  148.1 1.3 convolution_convert_fusion.5
  150.5 2.9 fusion.69
  153.3 8.0 %copy.24 = f32[8,8,128,256]{3,1,2,0:T(8,128)} copy(f32[8,8,128,256]{3,2,1,0:T(8,128)S(1)} %bitcast.81) | data formatting | bytes 16777216 | tf_op jit(solution)/shard_map/while
  161.3 13.2 %convolution_add_fusion.5 = f32[64,32768]{1,0:T(8,128)} fusion(f32[64,32768]{1,0:T(8,128)} %bitcast.83, f32[64,32768]{1,0:T(8,128)} %get-tuple-element.302, pred[]{:T(512)S(6)} %compare.6, f32[64]{0:T(128)S(1)} %fusion.70, s32[64]{0:T(128)S(1)} %get-tuple-element.282), kind=kOutput, calls=%fused_computation.4.clone.1 | convolution fusion | flops 1614815232 | bytes 25166336 | tf_op jit(solution)/shard_map/while/body/eval_jaxpr/dot_general | solution.py:29
  174.5 1.3 convolution_convert_fusion.5
  176.9 2.9 fusion.69
  179.8 8.0 %copy.24 = f32[8,8,128,256]{3,1,2,0:T(8,128)} copy(f32[8,8,128,256]{3,2,1,0:T(8,128)S(1)} %bitcast.81) | data formatting | bytes 16777216 | tf_op jit(solution)/shard_map/while
  187.7 13.2 %convolution_add_fusion.5 = f32[64,32768]{1,0:T(8,128)} fusion(f32[64,32768]{1,0:T(8,128)} %bitcast.83, f32[64,32768]{1,0:T(8,128)} %get-tuple-element.302, pred[]{:T(512)S(6)} %compare.6, f32[64]{0:T(128)S(1)} %fusion.70, s32[64]{0:T(128)S(1)} %get-tuple-element.282), kind=kOutput, calls=%fused_computation.4.clone.1 | convolution fusion | flops 1614815232 | bytes 25166336 | tf_op jit(solution)/shard_map/while/body/eval_jaxpr/dot_general | solution.py:29
  201.0 1.3 convolution_convert_fusion.5
  203.4 2.9 fusion.69
  206.3 8.0 %copy.24 = f32[8,8,128,256]{3,1,2,0:T(8,128)} copy(f32[8,8,128,256]{3,2,1,0:T(8,128)S(1)} %bitcast.81) | data formatting | bytes 16777216 | tf_op jit(solution)/shard_map/while
  214.2 13.2 %convolution_add_fusion.5 = f32[64,32768]{1,0:T(8,128)} fusion(f32[64,32768]{1,0:T(8,128)} %bitcast.83, f32[64,32768]{1,0:T(8,128)} %get-tuple-element.302, pred[]{:T(512)S(6)} %compare.6, f32[64]{0:T(128)S(1)} %fusion.70, s32[64]{0:T(128)S(1)} %get-tuple-element.282), kind=kOutput, calls=%fused_computation.4.clone.1 | convolution fusion | flops 1614815232 | bytes 25166336 | tf_op jit(solution)/shard_map/while/body/eval_jaxpr/dot_general | solution.py:29
  227.5 9.3 %reshape.45 = f32[8192,256]{1,0:T(8,128)} reshape(f32[64,32768]{1,0:T(8,128)} %get-tuple-element.98) | data formatting | bytes 16777216 | tf_op jit(solution)/shard_map/reshape | solution.py:45
  236.8 72.4 %reduce-scatter.3.cloned.1.call-done = f32[512,256]{1,0:T(8,128)} async-done(((f32[8192,256]{1,0:T(8,128)}), f32[512,256]{1,0:T(8,128)}) %reduce-scatter.3.cloned.1.call-update) | async-done | bytes 524304 | tf_op jit(solution)/shard_map/reduce_scatter | solution.py:75
  309.2 2.2 convert_reduce_fusion
  312.4 16.7 %copy.12 = bf16[1,384,128,128]{2,3,1,0:T(8,128)(2,1)} copy(bf16[1,384,128,128]{3,2,1,0:T(8,128)(2,1)} %bitcast.89) | data formatting | bytes 25165824 | tf_op args[4]
  330.2 18.4 %all-gather.5.cloned.1.call-done = bf16[8192,256]{1,0:T(8,128)(2,1)} async-done(((bf16[512,256]{1,0:T(8,128)(2,1)}), bf16[8192,256]{1,0:T(8,128)(2,1)}) %all-gather.5.cloned.1.call-update) | async-done | bytes 4194320 | tf_op jit(solution)/shard_map/all_gather | solution.py:79
  348.6 7.4 %reshape.46 = bf16[64,32768]{1,0:T(8,128)(2,1)} reshape(bf16[8192,256]{1,0:T(8,128)(2,1)} %all-gather.5.cloned.1.call-done) | data formatting | bytes 8388608 | tf_op jit(solution)/shard_map/reshape | solution.py:13
  356.0 142.7 %while.23 = (s32[]{:T(128)}, f32[32,32768]{1,0:T(8,128)}, s32[6,64]{1,0:T(8,128)S(1)}, pred[6,64]{1,0:T(8,128)(4,1)S(1)}, bf16[6,64,128,128]{2,3,1,0:T(8,128)(2,...) while((s32[]{:T(128)}, f32[32,32768]{1,0:T(8,128)}, ...), condition=%wide.region_4.5_spmd.clone, body=%wide.region_3.4_spmd.clone.sunk | while | flops 1614815232 | bytes 65014444 | solution.py:44
  356.0 3.5 convolution_convert_fusion.6
  360.6 2.9 fusion.77
  363.5 7.9 %copy.26 = f32[8,8,128,256]{3,1,2,0:T(8,128)} copy(f32[8,8,128,256]{3,2,1,0:T(8,128)S(1)} %bitcast.82) | data formatting | bytes 16777216 | tf_op jit(solution)/shard_map/while
  371.4 7.8 %convolution_add_fusion.6 = f32[32,32768]{1,0:T(8,128)} fusion(f32[64,32768]{1,0:T(8,128)} %bitcast.80, f32[32,32768]{1,0:T(8,128)} %get-tuple-element.329, pred[]{:T(512)S(6)} %compare.7, f32[64]{0:T(128)S(1)} %fusion.78, s32[64]{0:T(128)S(1)} %get-tuple-element.291), kind=kOutput, calls=%fused_computation.25.clone.1 | convolution fusion | flops 807407616 | bytes 16777728 | tf_op jit(solution)/shard_map/while/body/eval_jaxpr/dot_general | solution.py:29
  379.2 3.5 convolution_convert_fusion.6
  383.8 2.9 fusion.77
  386.7 7.9 %copy.26 = f32[8,8,128,256]{3,1,2,0:T(8,128)} copy(f32[8,8,128,256]{3,2,1,0:T(8,128)S(1)} %bitcast.82) | data formatting | bytes 16777216 | tf_op jit(solution)/shard_map/while
  394.6 8.5 %convolution_add_fusion.6 = f32[32,32768]{1,0:T(8,128)} fusion(f32[64,32768]{1,0:T(8,128)} %bitcast.80, f32[32,32768]{1,0:T(8,128)} %get-tuple-element.329, pred[]{:T(512)S(6)} %compare.7, f32[64]{0:T(128)S(1)} %fusion.78, s32[64]{0:T(128)S(1)} %get-tuple-element.291), kind=kOutput, calls=%fused_computation.25.clone.1 | convolution fusion | flops 807407616 | bytes 16777728 | tf_op jit(solution)/shard_map/while/body/eval_jaxpr/dot_general | solution.py:29
  403.1 3.5 convolution_convert_fusion.6
  407.7 2.9 fusion.77
  410.6 7.9 %copy.26 = f32[8,8,128,256]{3,1,2,0:T(8,128)} copy(f32[8,8,128,256]{3,2,1,0:T(8,128)S(1)} %bitcast.82) | data formatting | bytes 16777216 | tf_op jit(solution)/shard_map/while
  418.5 8.5 %convolution_add_fusion.6 = f32[32,32768]{1,0:T(8,128)} fusion(f32[64,32768]{1,0:T(8,128)} %bitcast.80, f32[32,32768]{1,0:T(8,128)} %get-tuple-element.329, pred[]{:T(512)S(6)} %compare.7, f32[64]{0:T(128)S(1)} %fusion.78, s32[64]{0:T(128)S(1)} %get-tuple-element.291), kind=kOutput, calls=%fused_computation.25.clone.1 | convolution fusion | flops 807407616 | bytes 16777728 | tf_op jit(solution)/shard_map/while/body/eval_jaxpr/dot_general | solution.py:29
  427.0 3.5 convolution_convert_fusion.6
  431.6 2.9 fusion.77
  434.5 7.9 %copy.26 = f32[8,8,128,256]{3,1,2,0:T(8,128)} copy(f32[8,8,128,256]{3,2,1,0:T(8,128)S(1)} %bitcast.82) | data formatting | bytes 16777216 | tf_op jit(solution)/shard_map/while
  442.4 8.5 %convolution_add_fusion.6 = f32[32,32768]{1,0:T(8,128)} fusion(f32[64,32768]{1,0:T(8,128)} %bitcast.80, f32[32,32768]{1,0:T(8,128)} %get-tuple-element.329, pred[]{:T(512)S(6)} %compare.7, f32[64]{0:T(128)S(1)} %fusion.78, s32[64]{0:T(128)S(1)} %get-tuple-element.291), kind=kOutput, calls=%fused_computation.25.clone.1 | convolution fusion | flops 807407616 | bytes 16777728 | tf_op jit(solution)/shard_map/while/body/eval_jaxpr/dot_general | solution.py:29
  450.9 3.5 convolution_convert_fusion.6
  455.5 2.9 fusion.77
  458.4 7.9 %copy.26 = f32[8,8,128,256]{3,1,2,0:T(8,128)} copy(f32[8,8,128,256]{3,2,1,0:T(8,128)S(1)} %bitcast.82) | data formatting | bytes 16777216 | tf_op jit(solution)/shard_map/while
  466.3 8.5 %convolution_add_fusion.6 = f32[32,32768]{1,0:T(8,128)} fusion(f32[64,32768]{1,0:T(8,128)} %bitcast.80, f32[32,32768]{1,0:T(8,128)} %get-tuple-element.329, pred[]{:T(512)S(6)} %compare.7, f32[64]{0:T(128)S(1)} %fusion.78, s32[64]{0:T(128)S(1)} %get-tuple-element.291), kind=kOutput, calls=%fused_computation.25.clone.1 | convolution fusion | flops 807407616 | bytes 16777728 | tf_op jit(solution)/shard_map/while/body/eval_jaxpr/dot_general | solution.py:29
  474.8 3.5 convolution_convert_fusion.6
  479.4 2.9 fusion.77
  482.3 7.9 %copy.26 = f32[8,8,128,256]{3,1,2,0:T(8,128)} copy(f32[8,8,128,256]{3,2,1,0:T(8,128)S(1)} %bitcast.82) | data formatting | bytes 16777216 | tf_op jit(solution)/shard_map/while
  490.2 8.5 %convolution_add_fusion.6 = f32[32,32768]{1,0:T(8,128)} fusion(f32[64,32768]{1,0:T(8,128)} %bitcast.80, f32[32,32768]{1,0:T(8,128)} %get-tuple-element.329, pred[]{:T(512)S(6)} %compare.7, f32[64]{0:T(128)S(1)} %fusion.78, s32[64]{0:T(128)S(1)} %get-tuple-element.291), kind=kOutput, calls=%fused_computation.25.clone.1 | convolution fusion | flops 807407616 | bytes 16777728 | tf_op jit(solution)/shard_map/while/body/eval_jaxpr/dot_general | solution.py:29
  498.7 4.9 reshape.47
  503.6 70.1 %psum.15 = f32[256]{0:T(256)S(1)} all-reduce(f32[256]{0:T(256)S(1)} %get-tuple-element.191), channel_id=1, replica_groups=mesh['row'=8,'col'=16] {'row','col'}, use_global_device_ids=true, to_apply=%region_8.9 | all-reduce | flops 256 | bytes 2048 | tf_op jit(solution)/shard_map/psum | solution.py:83
  574.3 1.7 broadcast_multiply_fusion
  576.0 13.0 %reduce-scatter.5.cloned.1.call-done = f32[512,256]{1,0:T(8,128)} async-done(((f32[4096,256]{1,0:T(8,128)}), f32[512,256]{1,0:T(8,128)}) %reduce-scatter.5.cloned.1.call-update) | async-done | bytes 524304 | tf_op jit(solution)/shard_map/reduce_scatter | solution.py:90
  589.1 1.8 convert_element_type.40
  (66 shorter events, 17.3 us)
Async XLA Ops:
  7.2 302.0 %copy-start = (bf16[256,256]{1,0:T(8,128)(2,1)S(1)}, bf16[256,256]{1,0:T(8,128)(2,1)}, u32[]{:S(2)}) copy-start(bf16[256,256]{1,0:T(8,128)(2,1)} %param.13) | copy-start | bytes 393220
  7.2 59.9 %all-gather.3.cloned.1.call-start = ((), (), s32[]{:S(2)}) async-start(), calls=%async_computation.2 | async-start | bytes 2359296 | tf_op jit(solution)/shard_map/all_gather | solution.py:71
  7.9 301.3 %reduce-scatter.3.cloned.1.call-start = ((), (), s32[]{:S(2)}) async-start(), calls=%async_computation.3 | async-start | bytes 8912896 | tf_op jit(solution)/shard_map/reduce_scatter | solution.py:75
  236.7 72.5 %copy-start.3 = (bf16[512,256]{1,0:T(8,128)(2,1)S(1)}, bf16[512,256]{1,0:T(8,128)(2,1)}, u32[]{:S(2)}) copy-start(bf16[512,256]{1,0:T(8,128)(2,1)} %param.15) | copy-start | bytes 786436
  236.7 72.5 %copy-start.4 = (f32[256]{0:T(256)S(1)}, f32[256]{0:T(256)}, u32[]{:S(2)}) copy-start(f32[256]{0:T(256)} %param.14) | copy-start | bytes 3076
  236.8 111.8 %all-gather.5.cloned.1.call-start = ((), (), s32[]{:S(2)}) async-start(), calls=%async_computation.4 | async-start | bytes 4456448 | tf_op jit(solution)/shard_map/all_gather | solution.py:79
  312.4 16.7 %copy-start.2 = (f32[512,256]{1,0:T(8,128)S(1)}, f32[512,256]{1,0:T(8,128)}, u32[]{:S(2)}) copy-start(f32[512,256]{1,0:T(8,128)} %reduce-scatter.3.cloned.1.call-done) | copy-start | bytes 1572868
  312.4 262.0 %all-reduce.2.cloned.1.call-start = ((), (), s32[]{:S(2)}) async-start(), calls=%async_computation.6 | async-start | bytes 524288 | tf_op jit(solution)/shard_map/psum | solution.py:83
  330.1 258.9 %reduce-scatter.5.cloned.1.call-start = ((), (), s32[]{:S(2)}) async-start(), calls=%async_computation.5 | async-start | bytes 4718592 | tf_op jit(solution)/shard_map/reduce_scatter | solution.py:90
  498.7 92.1 %copy-start.1 = (bf16[256,256]{1,0:T(8,128)(2,1)S(1)}, bf16[256,256]{1,0:T(8,128)(2,1)}, u32[]{:S(2)}) copy-start(bf16[256,256]{1,0:T(8,128)(2,1)} %param.13) | copy-start | bytes 393220
Sparse Core Ops, SparseCore 0:
  10.4 56.6 all-gather.2
  236.9 72.2 reduce-scatter.2
  312.5 36.0 all-gather.4
  353.7 142.0 all-reduce.1
  503.8 85.2 reduce-scatter.4
where the time goes:
time: 599 us; the launch traced here: 597 us
  matrix products  195 us (33%)
  waiting for transfers between devices  161 us (27%)
  local copies, waits for them, and re-layouts  150 us (25%)
  blocking collectives  70.1 us (12%)
  between operations  14.5 us (2%)
    dot_general x12, matrix products, group_step(): jnp.dot(place_table, product.reshape(group_size, block_edge * feature_wid...  128 us
    while x24, local copies, waits for them, and re-layouts  108 us
    reduce_scatter x1, waiting for transfers between devices, per_device(): lax.psum_scatter(partial_value, 'col', scatter_dimension=0, tiled=True)  72.4 us
    psum x1, blocking collectives, per_device(): weight_total, bias_total = lax.psum((weight_term, bias_sum), ('row', 'col'))  70.1 us
    all_gather x1, waiting for transfers between devices, per_device(): panel = lax.all_gather(features, 'row', axis=0, tiled=True)  56.8 us
    dot_general x12, matrix products, group_step(): jnp.einsum(einsum_form, group_vals, pieces, preferred_element_type=jnp.fl...  34.3 us
    dot_general x12, matrix products, group_step(): jnp.dot(pick_table, source_flat, preferred_element_type=jnp.float32)  28.6 us
    all_gather x1, waiting for transfers between devices, per_device(): group_grad = lax.all_gather(grad_mid, 'col', axis=0, tiled=True)  18.4 us
  transfers between devices with their start and end apart: 5, of which 4 were waited for; matrix products, arithmetic and copies ran while one was open for 30% of the time, Pallas kernels for 0%

commit v1 on v0

v1 whole, which is shorter than its diff:
```python
import functools

import jax
import jax.numpy as jnp
from jax import lax
from jax.experimental import pallas as pl
from jax.experimental.pallas import tpu as pltpu
from jax.sharding import PartitionSpec as P

BF16 = jnp.bfloat16
F32 = jnp.float32
I32 = jnp.int32

F = 256
BLK = 128
SLOTS = 384
STEP = 16
PAIRS = STEP // 2
LOAD = 32
GROUP = 64
PANEL = 32
MIB = 2**20

SMEM_SPEC = pl.BlockSpec(memory_space=pltpu.SMEM)
VMEM_SPEC = pl.BlockSpec(memory_space=pltpu.VMEM)
ANY_SPEC = pl.BlockSpec(memory_space=pl.ANY)


def column(row):
    return jnp.broadcast_to(row, (8, row.shape[1])).T[:, :1]


def sort_slots(unit, bounds, valid, target, source, zero_source, list_ref, tgt_ref):
    shift = unit.bit_length() - 1
    per_step = STEP // unit
    step_shift = per_step.bit_length() - 1
    count = bounds[-1]
    slot = lax.broadcasted_iota(I32, (1, SLOTS), 1)
    target = jnp.where(valid, target, 255)
    earlier = lax.broadcasted_iota(I32, (SLOTS, SLOTS), 0) < lax.broadcasted_iota(
        I32, (SLOTS, SLOTS), 1
    )
    targetf = target.astype(F32)
    same = (column(targetf) == targetf) & earlier
    rank = jnp.sum(jnp.where(same, 1.0, 0.0), axis=0, keepdims=True)
    ids = lax.broadcasted_iota(I32, (count, SLOTS), 0)
    tally = jnp.sum(jnp.where(ids == target, 1.0, 0.0), axis=1, keepdims=True)
    units = ((tally.astype(I32) + (unit - 1)) >> shift).astype(F32)
    offset = jnp.sum(jnp.where(ids < target, units, 0.0), axis=0, keepdims=True)
    local = target
    id_col = lax.broadcasted_iota(I32, (count, 1), 0)
    width = tgt_ref.shape[1]
    where_last = lax.broadcasted_iota(I32, (1, width), 1)
    tail = jnp.zeros((1, width), I32)
    for i, (low, high) in enumerate(zip(bounds, bounds[1:])):
        inside = (id_col >= low) & (id_col < high)
        total = jnp.sum(jnp.where(inside, units, 0.0), axis=0, keepdims=True)
        steps = (total.astype(I32) + (per_step - 1)) >> step_shift
        spare = (steps * per_step).astype(F32) - total
        offset = offset + jnp.where(target >= high, spare, 0.0)
        local = jnp.where((target >= low) & (target < high), target - low, local)
        tail = jnp.where(where_last == width - 4 + i, steps, tail)
    place = jnp.where(valid, unit * offset + rank, -1.0)
    place_col = column(place).astype(I32)
    entry_col = column((slot * 256 + source + 1).astype(F32))
    local_col = column(local.astype(F32))
    at = lax.broadcasted_iota(I32, (SLOTS, list_ref.shape[1]), 1)
    entry = jnp.sum(jnp.where(place_col == at, entry_col, 0.0), axis=0, keepdims=True)
    entry = entry.astype(I32)
    list_ref[...] = jnp.where(entry == 0, zero_source, entry - 1)
    at = lax.broadcasted_iota(I32, (SLOTS, width), 1)
    where = jnp.sum(jnp.where(place_col == unit * at, local_col, 0.0), axis=0, keepdims=True)
    tgt_ref[...] = jnp.where(where_last >= width - 4, tail, where.astype(I32))


def prep_kernel(meta, rows_hbm, cols_hbm, vals, *refs):
    list_a, tgt_a, list_b, tgt_b, held, rows, cols, sems, id_sems = refs
    live, y_hi, z, y_lo, x, core = [meta[i] for i in range(6)]
    ids = [
        pltpu.make_async_copy(rows_hbm, rows, id_sems.at[0]),
        pltpu.make_async_copy(cols_hbm, cols, id_sems.at[1]),
    ]
    chunks = [
        pltpu.make_async_copy(
            vals.at[pl.ds(LOAD * i, LOAD)], held.at[pl.ds(LOAD * i, LOAD)], sems.at[i]
        )
        for i in range(SLOTS // LOAD)
    ]
    for copy in ids:
        copy.start()
    for i, chunk in enumerate(chunks):
        pl.when(LOAD * i < live)(chunk.start)
    for copy in ids:
        copy.wait()

    row = rows[...]
    col = cols[...]
    used = lax.broadcasted_iota(I32, (1, SLOTS), 1) < live
    c = row >> 2
    dcore = (c & 1) ^ core
    dyl = (c >> 3) ^ y_lo
    dx = ((c >> 1) - x) & 3
    q = col >> 2
    dyh = (q >> 2) ^ y_hi
    dz = (q - z) & 3
    near = dyl * 3 + jnp.where(dx == 3, 2, dx)
    own = jnp.where(dx == 2, 32 + dyl * 4, 40 + near * 4)
    row_target = jnp.where(dcore == 1, dyl * 16 + dx * 4, own) + (row & 3)
    order = jnp.where(dz == 2, 0, jnp.where(dz == 0, 1, jnp.where(dz == 1, 2, 3)))
    col_target = jnp.where(dyh == 1, dz * 4, 16 + order * 4) + (col & 3)
    row_early = ((dyl == 0) & (dx != 2)) | ((dyl == 1) & (dx == 0))
    place = jnp.where(row_early, jnp.where(dyl == 1, 3, (dx + 1) >> 1), jnp.where(dyl == 1, dx, 0))
    row_source = dcore * 16 + place * 4 + (row & 3)
    col_early = (dyh == 0) & (dz != 2)
    place = jnp.where(col_early, (dz + 1) >> 1, jnp.where(dyh == 1, 1 + dz, 0))
    col_source = place * 4 + (col & 3)
    row_target = jnp.where(col_early, row_target, 64 + row_target)
    col_target = jnp.where(row_early, col_target, 32 + col_target)
    sort_slots(2, (0, 64, 96, 104, 128), used, row_target, col_source, 20, list_a, tgt_a)
    sort_slots(2, (0, 32, 48, 56, 64), used, col_target, row_source, 32, list_b, tgt_b)

    for i, chunk in enumerate(chunks):
        pl.when(LOAD * i < live)(chunk.wait)


def prep(meta, rows, cols, vals):
    tgts = pltpu.VMEM((1, 384), I32)
    return pl.pallas_call(
        prep_kernel,
        out_shape=(
            pltpu.VMEM((1, 640), I32),
            tgts,
            pltpu.VMEM((1, 640), I32),
            tgts,
            pltpu.VMEM((SLOTS, BLK, BLK), BF16),
        ),
        in_specs=[SMEM_SPEC] + [ANY_SPEC] * 3,
        out_specs=[VMEM_SPEC] * 5,
        scratch_shapes=[
            pltpu.VMEM((1, SLOTS), I32),
            pltpu.VMEM((1, SLOTS), I32),
            pltpu.SemaphoreType.DMA((SLOTS // LOAD,)),
            pltpu.SemaphoreType.DMA((2,)),
        ],
        compiler_params=pltpu.CompilerParams(vmem_limit_bytes=44 * MIB),
        cost_estimate=pl.CostEstimate(
            flops=2**20, bytes_accessed=SLOTS * BLK * BLK * 2, transcendentals=0
        ),
        name="slot_lists",
    )(meta, rows, cols, vals)


def start_pieces(places, pieces, field, sems):
    copies = [
        pltpu.make_async_copy(
            pieces[n].at[pl.ds(first, size)], field.at[pl.ds(to, size)], sems.at[i]
        )
        for i, (n, first, size, to) in enumerate(places)
    ]
    for copy in copies:
        copy.start()
    return copies


PANEL_EARLY = [(0, 0, 4, 0), (1, 0, 4, 4), (2, 0, 4, 8)]
PANEL_LATE = [
    (0, 0, 2, 0),
    (1, 0, 2, 2),
    (2, 0, 4, 4),
    (3, 0, 4, 8),
    (4, 0, 2, 12),
    (5, 0, 2, 14),
    (6, 0, 4, 16),
]
GROUP_EARLY = [(0, 0, 4, 0), (1, 0, 4, 4), (2, 0, 4, 8), (3, 0, 4, 12), (4, 0, 4, 16), (5, 0, 12, 20)]
GROUP_LATE = [
    (0, 0, 4, 4),
    (0, 4, 2, 0),
    (1, 0, 4, 12),
    (1, 4, 2, 2),
    (2, 0, 2, 8),
    (3, 0, 2, 10),
    (4, 0, 4, 20),
    (4, 4, 2, 16),
    (4, 6, 4, 28),
    (4, 10, 2, 18),
    (5, 0, 4, 24),
]


def block_loop(part, forward, list_ref, tgt_ref, held, field, acc):
    tail = tgt_ref.shape[1] - 4
    first = 0
    for i in range(part):
        first = first + tgt_ref[0, tail + i]

    def body(step, _):
        for p in range(PAIRS):
            entries = [list_ref[0, step * STEP + p * 2 + u] for u in range(2)]
            t = tgt_ref[0, step * PAIRS + p]
            blocks = [held[e >> 8] for e in entries]
            fields = [field[e & 255] for e in entries]
            lhs, rhs = (blocks, fields) if forward else (fields, blocks)
            acc[t] += jnp.dot(
                jnp.concatenate(lhs, axis=1),
                jnp.concatenate(rhs, axis=0),
                preferred_element_type=F32,
            )
        return 0

    lax.fori_loop(first, first + tgt_ref[0, tail + part], body, 0)


def clear(acc):
    def step(t, _):
        acc[t] = jnp.zeros(acc.shape[1:], F32)
        return 0

    lax.fori_loop(0, acc.shape[0], step, 0)


def take_over(acc, early, first):
    def step(t, _):
        acc[t] = early[first + t]
        return 0

    lax.fori_loop(0, acc.shape[0], step, 0)


def early_kernel(places, forward, list_ref, tgt_ref, held, *refs):
    *pieces, sums, field, sems = refs
    copies = start_pieces(places, pieces, field, sems)
    last = field.shape[0] - 1
    field[last] = jnp.zeros(field.shape[1:], BF16)
    clear(sums)
    for copy in copies:
        copy.wait()
    block_loop(0, forward, list_ref, tgt_ref, held, field, sums)


def early_product(places, forward, name, sums, field, lists, tgts, held, pieces):
    return pl.pallas_call(
        functools.partial(early_kernel, places, forward),
        out_shape=pltpu.VMEM(sums, F32),
        in_specs=[SMEM_SPEC] * 2 + [VMEM_SPEC] + [ANY_SPEC] * len(pieces),
        out_specs=VMEM_SPEC,
        scratch_shapes=[pltpu.VMEM(field, BF16), pltpu.SemaphoreType.DMA((20,))],
        compiler_params=pltpu.CompilerParams(vmem_limit_bytes=8 * MIB),
        cost_estimate=pl.CostEstimate(
            flops=SLOTS * BLK * BLK * F, bytes_accessed=12 * MIB, transcendentals=0
        ),
        name=name,
    )(lists, tgts, held, *pieces)


def gather_field(places, pieces, field, acc, early, sems):
    copies = start_pieces(places, pieces, field, sems)
    last = field.shape[0] - 1
    field[last] = jnp.zeros(field.shape[1:], BF16)
    take_over(acc, early, 0)
    for copy in copies:
        copy.wait()


def product_call(kernel, name, out_shape, acc_shape, pieces, args):
    count = len(pieces)
    scratch = [pltpu.VMEM(acc_shape, F32)] if acc_shape else []
    if count:
        scratch.append(pltpu.SemaphoreType.DMA((20,)))
    lists, tgts, held, *fields = args
    return pl.pallas_call(
        kernel,
        out_shape=out_shape,
        in_specs=[SMEM_SPEC] * 2
        + [VMEM_SPEC] * (1 + len(fields))
        + [ANY_SPEC] * count,
        out_specs=[VMEM_SPEC] * len(out_shape),
        scratch_shapes=scratch,
        compiler_params=pltpu.CompilerParams(vmem_limit_bytes=10 * MIB),
        cost_estimate=pl.CostEstimate(
            flops=SLOTS * BLK * BLK * F, bytes_accessed=12 * MIB, transcendentals=0
        ),
        name=name,
    )(lists, tgts, held, *fields, *pieces)


def forward_other_kernel(list_ref, tgt_ref, held, early, *refs):
    *pieces, far, near, field, acc, sems = refs
    gather_field(PANEL_LATE, pieces, field, acc, early, sems)
    block_loop(1, True, list_ref, tgt_ref, held, field, acc)

    def store(i, _):
        for dy in range(2):
            far[dy, i] = acc[16 * dy + 8 + i].astype(BF16)
            for n, dx in enumerate((0, 1, 3)):
                near[dy, n, i] = acc[16 * dy + 4 * dx + i].astype(BF16)
        return 0

    lax.fori_loop(0, 4, store, 0)


def forward_other(lists, tgts, held, early, pieces):
    return product_call(
        forward_other_kernel,
        "forward_other_core",
        (
            jax.ShapeDtypeStruct((2, 4, BLK, F), BF16),
            jax.ShapeDtypeStruct((2, 3, 4, BLK, F), BF16),
            pltpu.VMEM((21, BLK, F), BF16),
        ),
        (32, BLK, F),
        pieces,
        (lists, tgts, held, early),
    )


def forward_own_kernel(part, list_ref, tgt_ref, held, early, field, sums):
    take_over(sums, early, (32, 40)[part])
    block_loop(part + 2, True, list_ref, tgt_ref, held, field, sums)


def forward_own(part, lists, tgts, held, early, field):
    return product_call(
        functools.partial(forward_own_kernel, part),
        ("forward_own_far", "forward_own_near")[part],
        (jax.ShapeDtypeStruct(((8, 24)[part], BLK, F), F32),),
        None,
        (),
        (lists, tgts, held, early, field),
    )[0]


WHOLE = jax.ShapeDtypeStruct((4, F, BLK), BF16)
WHOLE_SUM = jax.ShapeDtypeStruct((4, F, BLK), F32)
HALF = jax.ShapeDtypeStruct((2, F, BLK), BF16)


def backward_across_kernel(list_ref, tgt_ref, held, early, *refs):
    *pieces, own, up, down, low, high, field, acc, sems = refs
    gather_field(GROUP_LATE, pieces, field, acc, early, sems)
    block_loop(1, False, list_ref, tgt_ref, held, field, acc)

    def store(i, _):
        own[i] = acc[i]
        up[i] = acc[4 + i].astype(BF16)
        down[i] = acc[12 + i].astype(BF16)
        return 0

    lax.fori_loop(0, 4, store, 0)
    for i in range(2):
        low[i] = acc[8 + i].astype(BF16)
        high[i] = acc[10 + i].astype(BF16)


def backward_across(lists, tgts, held, early, pieces):
    return product_call(
        backward_across_kernel,
        "backward_across",
        (WHOLE_SUM, WHOLE, WHOLE, HALF, HALF, pltpu.VMEM((33, F, BLK), BF16)),
        (16, F, BLK),
        pieces,
        (lists, tgts, held, early),
    )


def backward_far_kernel(list_ref, tgt_ref, held, early, field, low, high, own, acc):
    take_over(acc, early, 16)
    block_loop(2, False, list_ref, tgt_ref, held, field, acc)
    for i in range(2):
        low[i] = acc[i].astype(BF16)
        high[i] = acc[2 + i].astype(BF16)
    for i in range(4):
        own[i] = acc[4 + i]


def backward_far(lists, tgts, held, early, field):
    return product_call(
        backward_far_kernel,
        "backward_far_own",
        (HALF, HALF, WHOLE_SUM),
        (8, F, BLK),
        (),
        (lists, tgts, held, early, field),
    )


def backward_near_kernel(list_ref, tgt_ref, held, early, field, up, down, acc):
    take_over(acc, early, 24)
    block_loop(3, False, list_ref, tgt_ref, held, field, acc)
    for i in range(4):
        up[i] = acc[i].astype(BF16)
        down[i] = acc[4 + i].astype(BF16)


def backward_near(lists, tgts, held, early, field):
    return product_call(
        backward_near_kernel,
        "backward_near",
        (WHOLE, WHOLE),
        (8, F, BLK),
        (),
        (lists, tgts, held, early, field),
    )


def dense_kernel(norm, *refs):
    parts = refs[:4]
    weight, bias, upstream, activation, mid, terms = refs[4:]
    w = weight[...]
    w_term = jnp.zeros((F, F), F32)
    b_term = jnp.zeros((1, F), F32)
    for i in range(4):
        rows = pl.ds(BLK * i, BLK)
        total = parts[0][0, i]
        for part in parts[1:]:
            total = total + part[i].astype(F32)
        aggregated = total.astype(BF16)
        preact = jnp.dot(aggregated, w, preferred_element_type=F32) + bias[...]
        sig = jax.nn.sigmoid(preact)
        activation[rows, :] = (preact * sig).astype(BF16)
        grad_pre = (
            upstream[rows, :].astype(F32) * sig * (1.0 + preact * (1.0 - sig))
        ).astype(BF16)
        mid[i] = lax.dot_general(
            w, grad_pre, (((1,), (1,)), ((), ())), preferred_element_type=F32
        ).astype(BF16)
        w_term += lax.dot_general(
            aggregated, grad_pre, (((0,), (0,)), ((), ())), preferred_element_type=F32
        )
        b_term += jnp.sum(grad_pre.astype(F32), axis=0, keepdims=True)
    terms[pl.ds(0, F), :] = w_term * norm
    terms[pl.ds(F, 8), :] = jnp.broadcast_to(b_term * norm, (8, F))


def dense(parts, weight, bias, upstream, norm):
    return pl.pallas_call(
        functools.partial(dense_kernel, norm),
        out_shape=(
            jax.ShapeDtypeStruct((4 * BLK, F), BF16),
            jax.ShapeDtypeStruct((4, F, BLK), BF16),
            jax.ShapeDtypeStruct((F + 8, F), F32),
        ),
        in_specs=[VMEM_SPEC] * 7,
        out_specs=[VMEM_SPEC] * 3,
        compiler_params=pltpu.CompilerParams(vmem_limit_bytes=12 * MIB),
        cost_estimate=pl.CostEstimate(
            flops=6 * 512 * F * F, bytes_accessed=4 * 2**20, transcendentals=512 * F
        ),
        name="dense_layer",
    )(*parts, weight, bias.reshape(1, F), upstream)


def across_kernel(own, across, out):
    for i in range(4):
        out[i] = own[i] + across[i].astype(F32)


def add_across(own, across):
    return pl.pallas_call(
        across_kernel,
        out_shape=jax.ShapeDtypeStruct(own.shape, F32),
        in_specs=[VMEM_SPEC] * 2,
        out_specs=VMEM_SPEC,
        compiler_params=pltpu.CompilerParams(vmem_limit_bytes=8 * MIB),
        cost_estimate=pl.CostEstimate(flops=10**10, bytes_accessed=MIB, transcendentals=0),
        name="add_across",
    )(own, across)


def finish_kernel(here, up, down, mine, theirs, grad, w_grad, b_grad):
    for i in range(4):
        total = here[i] + (up[i].astype(F32) + down[i].astype(F32))
        grad[pl.ds(BLK * i, BLK), :] = total.T.astype(BF16)
    total = mine[...].astype(F32) + theirs[...].astype(F32)
    w_grad[...] = total[:F]
    b_grad[...] = total[F : F + 1]


def finish(here, up, down, mine, theirs):
    return pl.pallas_call(
        finish_kernel,
        out_shape=(
            jax.ShapeDtypeStruct((4 * BLK, F), BF16),
            jax.ShapeDtypeStruct((F, F), F32),
            jax.ShapeDtypeStruct((1, F), F32),
        ),
        in_specs=[VMEM_SPEC] * 5,
        out_specs=[VMEM_SPEC] * 3,
        compiler_params=pltpu.CompilerParams(vmem_limit_bytes=8 * MIB),
        name="finish_grads",
    )(here, up, down, mine, theirs)


def halves_kernel(*refs):
    up, down, low, high = refs[:4]
    up_out, down_out = refs[-2:]
    for i in range(2):
        up_out[i] = (up[i].astype(F32) + low[i].astype(F32)).astype(BF16)
        up_out[2 + i] = up[2 + i]
        down_out[i] = down[i]
        down_out[2 + i] = (down[2 + i].astype(F32) + high[i].astype(F32)).astype(BF16)
        for extra, out in zip(refs[4:-2], refs[-2:]):
            out[4 + i] = extra[i]


def add_halves(up, down, low, high, *extras):
    blocks = 6 if extras else 4
    return pl.pallas_call(
        halves_kernel,
        out_shape=[jax.ShapeDtypeStruct((blocks, *up.shape[1:]), BF16)] * 2,
        in_specs=[VMEM_SPEC] * (4 + len(extras)),
        out_specs=[VMEM_SPEC] * 2,
        compiler_params=pltpu.CompilerParams(vmem_limit_bytes=8 * MIB),
        cost_estimate=pl.CostEstimate(flops=2**18, bytes_accessed=MIB, transcendentals=0),
        name="add_halves",
    )(up, down, low, high, *extras)


def relay_kernel(keep, got, low, high, up1, down1, up0, down0, own):
    for dy, up, down in ((1, up1, down1), (0, up0, down0)):
        for i in range(4):
            at = 12 * dy + i
            own[dy, i] = keep[at] + got[dy, 0, i].astype(F32)
            right = keep[at + 4] + got[dy, 1, i].astype(F32)
            left = keep[at + 8] + got[dy, 2, i].astype(F32)
            if i < 2:
                right = right + low[dy, i].astype(F32)
            else:
                left = left + high[dy, i - 2].astype(F32)
            up[i] = right.astype(BF16)
            down[i] = left.astype(BF16)


def relay(keep, got, low, high):
    return pl.pallas_call(
        relay_kernel,
        out_shape=[jax.ShapeDtypeStruct((4, BLK, F), BF16)] * 4
        + [jax.ShapeDtypeStruct((2, 4, BLK, F), F32)],
        in_specs=[VMEM_SPEC] * 4,
        out_specs=[VMEM_SPEC] * 5,
        compiler_params=pltpu.CompilerParams(vmem_limit_bytes=8 * MIB),
        cost_estimate=pl.CostEstimate(flops=2**21, bytes_accessed=6 * MIB, transcendentals=0),
        name="relay_sums",
    )(keep, got, low, high)


def from_row(value, dy, dz):
    perm = [((((q >> 2) ^ dy) * 4 + ((q + dz) & 3)), q) for q in range(8)]
    return lax.ppermute(value, "row", perm)


def col_peer(c, dcore, dy, dx):
    return ((c >> 3) ^ dy) * 8 + ((((c >> 1) & 3) + dx) & 3) * 2 + ((c & 1) ^ dcore)


def from_col(value, dcore, dy, dx):
    return lax.ppermute(value, "col", [(col_peer(c, dcore, dy, dx), c) for c in range(16)])


def tie(*values):
    return lax.optimization_barrier(values)


def join(*pieces):
    return jnp.concatenate(pieces, axis=0)


def per_device(
    features, weight, bias_term, upstream, block_values, block_rows, block_cols, live_count
):
    vals = block_values.reshape(SLOTS, BLK, BLK)
    row = lax.axis_index("row")
    col = lax.axis_index("col")
    meta = jnp.stack(
        [live_count[0, 0], row >> 2, row & 3, col >> 3, (col >> 1) & 3, col & 1, row, col]
    ).astype(I32)
    list_a, tgt_a, list_b, tgt_b, held = prep(meta, block_rows, block_cols, vals)

    shard = features.reshape(4, BLK, F)
    other = from_row(shard, 1, 0)
    up, down = from_row(shard, 0, 1), from_row(shard, 0, 3)
    up, down, other, list_a = tie(up, down, other, list_a)
    up2, down2 = from_row(other, 0, 1), from_row(other, 0, 3)
    late = [from_row(up[:2], 0, 1), from_row(down[2:], 0, 3), other]
    early = early_product(
        PANEL_EARLY,
        True,
        "forward_early",
        (64, BLK, F),
        (21, BLK, F),
        list_a,
        tgt_a,
        held,
        (shard, up, down),
    )
    up2, down2, early = tie(up2, down2, early)
    late += [up2, from_row(up2[:2], 0, 1), from_row(down2[2:], 0, 3), down2]

    send_far, send_near, field = forward_other(list_a, tgt_a, held, early, late)
    got_far = from_col(send_far, 1, 0, 0)
    got_near = from_col(send_near, 1, 0, 0)
    keep_far = forward_own(0, list_a, tgt_a, held, early, field)
    far = (keep_far.reshape(2, 4, BLK, F) + got_far.astype(F32)).astype(BF16)
    low, high = far[:, :2], far[:, 2:]
    list_a2, low, high = tie(list_a, low, high)
    low, high = from_col(low, 0, 0, 3), from_col(high, 0, 0, 1)
    keep_near = forward_own(1, list_a2, tgt_a, held, early, field)
    up1, down1, up0, down0, own = relay(keep_near, got_near, low, high)
    up1, down1 = from_col(up1, 0, 0, 3), from_col(down1, 0, 0, 1)
    across = (own[1] + up1.astype(F32) + down1.astype(F32)).astype(BF16)
    up0, down0, across = tie(up0, down0, across)
    across = from_col(across, 0, 1, 0)
    up0, down0 = from_col(up0, 0, 0, 3), from_col(down0, 0, 0, 1)

    nodes = 4 * BLK * lax.axis_size("row") * lax.axis_size("col")
    activation, mid, terms = dense(
        [own, up0, down0, across], weight, bias_term, upstream, float(nodes) ** -0.5
    )

    def pair(value, axis, kind, bit):
        value = value.astype(kind)
        peers = [(i ^ bit, i) for i in range(lax.axis_size(axis))]
        return value, lax.ppermute(value, axis, peers)

    def add(mine, theirs):
        return mine.astype(F32) + theirs.astype(F32)

    def core(value):
        return from_col(value, 1, 0, 0)

    up, down = from_col(mid, 0, 0, 1), from_col(mid, 0, 0, 3)
    other = from_col(mid, 0, 1, 0)
    terms1 = add(*pair(terms, "col", F32, 1))
    other, terms1 = tie(other, terms1)
    mine, theirs = pair(terms1, "row", F32, 1)
    up2 = from_col(join(other, up[:2]), 0, 0, 1)
    down2 = from_col(join(other, down[2:]), 0, 0, 3)
    mates = [core(mid), core(join(up, down, other))]
    early = early_product(
        GROUP_EARLY,
        False,
        "backward_early",
        (32, F, BLK),
        (33, F, BLK),
        list_b,
        tgt_b,
        held,
        (mid, up, down, other, *mates),
    )
    up2, down2, theirs, early = tie(up2, down2, theirs, early)
    up2, down2, terms2 = tie(up2, down2, add(mine, theirs))
    mine, theirs = pair(terms2, "col", F32, 8)
    low, high = from_col(up2[:2], 0, 0, 1), from_col(down2[2:4], 0, 0, 3)
    late = [up2, down2, low, high, core(join(up2, down2)), core(join(low, high))]
    list_b1, terms3 = tie(list_b, add(mine, theirs))
    mine, theirs = pair(terms3, "row", BF16, 2)

    own1, up1, down1, low1, high1, field = backward_across(list_b1, tgt_b, held, early, late)
    theirs, own1 = tie(theirs, own1)
    terms4 = add(mine, theirs)
    low1, high1 = from_row(low1, 0, 3), from_row(high1, 0, 1)
    mine, theirs = pair(terms4, "row", BF16, 4)
    low0, high0, own0 = backward_far(list_b, tgt_b, held, early, field)
    up1, down1, own0 = tie(up1, down1, own0)
    up1, down1 = add_halves(up1, down1, low1, high1, low0, high0)
    theirs, up1, down1 = tie(theirs, up1, down1)
    list_b2, terms5 = tie(list_b, add(mine, theirs))
    up1, down1 = from_row(up1, 0, 3), from_row(down1, 0, 1)
    mine, theirs = pair(terms5, "col", BF16, 2)
    up0, down0 = backward_near(list_b2, tgt_b, held, early, field)
    up1, down1, up0, theirs = tie(up1, down1, up0, theirs)
    across = (own1 + up1[:4].astype(F32) + down1[:4].astype(F32)).astype(BF16)
    across = from_row(across, 1, 0)
    up0, down0 = add_halves(up0, down0, up1[4:], down1[4:])
    up0, down0 = from_row(up0, 0, 3), from_row(down0, 0, 1)
    mine, theirs = pair(add(mine, theirs), "col", BF16, 4)
    here = add_across(own0, across)
    feature_grad, weight_grad, bias_grad = finish(here, up0, down0, mine, theirs)
    return (activation, feature_grad, weight_grad, bias_grad.reshape(F))


def solution(mesh):
    in_specs = (
        P(("row", "col"), None),
        P(),
        P(),
        P(("row", "col"), None),
        P("row", "col", None, None),
        P("row", "col"),
        P("row", "col"),
        P("row", "col"),
    )
    out_specs = (P(("row", "col"), None), P(("row", "col"), None), P(), P())
    return jax.shard_map(
        per_device, mesh=mesh, in_specs=in_specs, out_specs=out_specs, check_vma=False
    )
```

time: 599 us -> 146 us (0.24)
  matrix products: 195 us -> 0 us
  local copies, waits for them, and re-layouts: 150 us -> 0.84 us
  waiting for transfers between devices: 161 us -> 55.1 us
  blocking collectives: 70.1 us -> 0 us
  starting transfers between devices: 0.2 us -> 60.1 us
  Pallas kernels: 0 us -> 27 us
  between operations: 14.5 us -> 1.64 us
    dot_general x39 -> x0, matrix products: 195 us -> none  [the longest x12 128 us: group_step(): jnp.dot(place_table, product.reshape(group_size, block_edge * feature_wid...]
    while x24 -> x0, local copies, waits for them, and re-layouts: 108 us -> none
    reduce_scatter x2 -> x0, waiting for transfers between devices: 85.4 us -> none  [the longest x1 72.4 us: per_device(): lax.psum_scatter(partial_value, 'col', scatter_dimension=0, tiled=True)]
    all_gather x2 -> x0, waiting for transfers between devices: 75.2 us -> none  [the longest x1 56.8 us: per_device(): panel = lax.all_gather(features, 'row', axis=0, tiled=True)]
    psum x1 -> x0, blocking collectives: 70.1 us -> none  [per_device(): weight_total, bias_total = lax.psum((weight_term, bias_sum), ('row', 'col'))]
    ppermute x0 -> x43, starting transfers between devices: none -> 60.1 us  [the longest x16 28.7 us: from_row(): return lax.ppermute(value, 'row', perm)]
    ppermute x0 -> x43, waiting for transfers between devices: none -> 55.1 us  [the longest x20 29.2 us: from_col(): lax.ppermute(value, 'col', [(col_peer(c, dcore, dy, dx), c) for c in rang...]
    pallas_call x0 -> x15, Pallas kernels: none -> 27 us  [the longest x6 13 us: product_call(): pl.pallas_call(kernel, out_shape=out_shape, in_specs=[SMEM_SPEC] * 2 + [V...]
  transfers between devices with their start and end apart: 5 -> 43, of which waited for: 4 -> 22; matrix products, arithmetic and copies ran while one was open for 30% -> 1% of each run, Pallas kernels for 0% -> 14%
where the time goes in v1:
time: 146 us; the launch traced here: 145 us
  starting transfers between devices  60.1 us (41%)
  waiting for transfers between devices  55.1 us (38%)
  Pallas kernels  27 us (18%)
  between operations  1.64 us (1%)
    ppermute x20, waiting for transfers between devices, from_col(): lax.ppermute(value, 'col', [(col_peer(c, dcore, dy, dx), c) for c in rang...  29.2 us
    ppermute x16, starting transfers between devices, from_row(): return lax.ppermute(value, 'row', perm)  28.7 us
    ppermute x20, starting transfers between devices, from_col(): lax.ppermute(value, 'col', [(col_peer(c, dcore, dy, dx), c) for c in rang...  25.8 us
    ppermute x7, waiting for transfers between devices, pair(): return (value, lax.ppermute(value, axis, peers))  17.6 us
    pallas_call x6, Pallas kernels, product_call(): pl.pallas_call(kernel, out_shape=out_shape, in_specs=[SMEM_SPEC] * 2 + [V...  13 us
    ppermute x16, waiting for transfers between devices, from_row(): return lax.ppermute(value, 'row', perm)  8.25 us
    pallas_call x2, Pallas kernels, early_product(): pl.pallas_call(functools.partial(early_kernel, places, forward), out_shap...  6.51 us
    ppermute x7, starting transfers between devices, pair(): return (value, lax.ppermute(value, axis, peers))  5.62 us
  transfers between devices with their start and end apart: 43, of which 22 were waited for; matrix products, arithmetic and copies ran while one was open for 1% of the time, Pallas kernels for 14%

profile of v1, /device:TPU:0, one launch (start us, length us, event | category | flops | bytes accessed | tf_op | source)
XLA Modules:
  0.0 145.5 jit_solution(14306002366227404183)
XLA Ops:
  0.6 3.4 %collective-permute-start.2 = (bf16[4,128,256]{2,1,0:T(8,128)(2,1)}, bf16[4,128,256]{2,1,0:T(8,128)(2,1)S(1)}, u32[]{:S(2)}, u32[]{:S(2)}) collective-permute-start(bf16[4,128,256]{2,1,0:T(8,128)(2,1)} %bitcast.21), channel_id=1, source_target_pairs={{64,0},{80,16},{96,32},{112,48},{0,64},{16,80},{32,96},{48,112},{6... | collective-permute-start | bytes 786440 | tf_op jit(solution)/shard_map/ppermute | solution.py:549
  4.0 1.9 %collective-permute-start.1 = (bf16[4,128,256]{2,1,0:T(8,128)(2,1)}, bf16[4,128,256]{2,1,0:T(8,128)(2,1)S(1)}, u32[]{:S(2)}, u32[]{:S(2)}) collective-permute-start(bf16[4,128,256]{2,1,0:T(8,128)(2,1)} %bitcast.22), channel_id=1, source_target_pairs={{48,0},{0,16},{16,32},{32,48},{112,64},{64,80},{80,96},{96,112},{4... | collective-permute-start | bytes 786440 | tf_op jit(solution)/shard_map/ppermute | solution.py:549
  5.9 2.1 %collective-permute-start = (bf16[4,128,256]{2,1,0:T(8,128)(2,1)}, bf16[4,128,256]{2,1,0:T(8,128)(2,1)S(1)}, u32[]{:S(2)}, u32[]{:S(2)}) collective-permute-start(bf16[4,128,256]{2,1,0:T(8,128)(2,1)} %bitcast.23), channel_id=1, source_target_pairs={{16,0},{32,16},{48,32},{0,48},{80,64},{96,80},{112,96},{64,112},{1... | collective-permute-start | bytes 786440 | tf_op jit(solution)/shard_map/ppermute | solution.py:549
  8.7 0.7 stack.31.meta
  9.4 4.4 %slot_lists.1 = (s32[1,640]{1,0:T(1,128)S(1)}, s32[1,384]{1,0:T(1,128)S(1)}, s32[1,640]{1,0:T(1,128)S(1)}, s32[1,384]{1,0:T(1,128)S(1)}, bf16[384,128,128]{2,1,0:T(8,128)(2,1)S(1)}) custom-call(s32[8]{0:T(128)} %stack.31.meta, s32[1,384]{1,0:T(1,128)} %rows_hbm.1, s32[1,384]{1,0:T(1,128)} %cols_hbm.1, bf16[384,128,128]{2,1,0:T(8,128)(2,1)} %bitcast.26), custom_call_target="tpu_custom_call" | custom-call | flops 1048576 | bytes 12582912 | tf_op jit(solution)/shard_map/slot_lists/pallas_call | solution.py:128
  13.8 0.5 collective-permute-done.1.refs_2_
  14.3 1.2 collective-permute-start.4
  15.5 2.0 %collective-permute-start.3 = (bf16[4,128,256]{2,1,0:T(8,128)(2,1)S(1)}, bf16[4,128,256]{2,1,0:T(8,128)(2,1)S(1)}, u32[]{:S(2)}, u32[]{:S(2)}) collective-permute-start(bf16[4,128,256]{2,1,0:T(8,128)(2,1)S(1)} %collective-permute-done.2.refs_2_), channel_id=1, source_target_pairs={{16,0},{32,16},{48,32},{0,48},{80,64},{96,80},{112,96},{64,112},{1... | collective-permute-start | bytes 786440 | tf_op jit(solution)/shard_map/ppermute | solution.py:549
  17.6 3.2 %collective-permute-start.5 = (bf16[2,128,256]{2,1,0:T(8,128)(2,1)S(1)}, bf16[2,128,256]{2,1,0:T(8,128)(2,1)S(1)}, u32[]{:S(2)}, u32[]{:S(2)}) collective-permute-start(bf16[2,128,256]{2,1,0:T(8,128)(2,1)S(1)} %slice.45), channel_id=1, source_target_pairs={{16,0},{32,16},{48,32},{0,48},{80,64},{96,80},{112,96},{64,112},{1... | collective-permute-start | bytes 393224 | tf_op jit(solution)/shard_map/ppermute | solution.py:549
  20.9 3.1 %forward_early.1.early = f32[64,128,256]{2,1,0:T(8,128)S(1)} custom-call(s32[1,640]{1,0:T(1,128)S(1)} %get-tuple-element.88.list_ref, s32[1,384]{1,0:T(1,128)S(1)} %get-tuple-element.78.tgt_ref, bf16[384,128,128]{2,1,0:T(8,128)(2,1)S(1)} %get-tuple-element.79.held, bf16[4,128,256]{2,1,0:T(8,128)(2,1)S(1)} %bitcast.24, ...), custom_call_target="tpu_custom_call" | custom-call | flops 1610612736 | bytes 12582912 | tf_op jit(solution)/shard_map/forward_early/pallas_call | solution.py:242
  24.1 1.2 collective-permute-start.8
  25.3 2.1 %collective-permute-start.7 = (bf16[2,128,256]{2,1,0:T(8,128)(2,1)S(1)}, bf16[2,128,256]{2,1,0:T(8,128)(2,1)S(1)}, u32[]{:S(2)}, u32[]{:S(2)}) collective-permute-start(bf16[2,128,256]{2,1,0:T(8,128)(2,1)S(1)} %slice.47), channel_id=1, source_target_pairs={{16,0},{32,16},{48,32},{0,48},{80,64},{96,80},{112,96},{64,112},{1... | collective-permute-start | bytes 393224 | tf_op jit(solution)/shard_map/ppermute | solution.py:549
  27.4 2.9 %collective-permute-done.8.refs_5_ = bf16[2,128,256]{2,1,0:T(8,128)(2,1)S(1)} collective-permute-done((bf16[2,128,256]{2,1,0:T(8,128)(2,1)S(1)}, bf16[2,128,256]{2,1,0:T(8,128)(2,1)S(1)}, u32[]{:S(2)}, u32[]{:S(2)}) %collective-permute-start.8) | collective-permute-done | bytes 131104 | tf_op jit(solution)/shard_map/ppermute | solution.py:549
  30.4 3.4 %forward_other_core.1 = (bf16[2,4,128,256]{3,2,1,0:T(8,128)(2,1)S(1)}, bf16[2,3,4,128,256]{4,3,2,1,0:T(8,128)(2,1)S(1)}, bf16[21,128,256]{2,1,0:T(8,128)(2,1)S(1)}) custom-call(s32[1,640]{1,0:T(1,128)S(1)} %get-tuple-element.88.list_ref, s32[1,384]{1,0:T(1,128)S(1)} %get-tuple-element.78.tgt_ref, bf16[384,128,128]{2,1,0:T(8,128)(2,1)S(1)} %get-tuple-element.79.held, ...), custom_call_target="tpu_custom_call" | custom-call | flops 1610612736 | bytes 12582912 | tf_op jit(solution)/shard_map/forward_other_core/pallas_call | solution.py:271
  33.8 0.5 collective-permute-start.9
  34.3 1.0 forward_own_far.1
  35.4 2.6 %collective-permute-done.9 = bf16[2,4,128,256]{3,2,1,0:T(8,128)(2,1)S(1)} collective-permute-done((bf16[2,4,128,256]{3,2,1,0:T(8,128)(2,1)S(1)}, bf16[2,4,128,256]{3,2,1,0:T(8,128)(2,1)S(1)}, u32[]{:S(2)}, u32[]{:S(2)}) %collective-permute-start.9) | collective-permute-done | bytes 524320 | tf_op jit(solution)/shard_map/ppermute | solution.py:557
  38.2 3.9 %collective-permute-start.11 = (bf16[2,2,128,256]{3,2,1,0:T(8,128)(2,1)S(1)}, bf16[2,2,128,256]{3,2,1,0:T(8,128)(2,1)S(1)}, u32[]{:S(2)}, u32[]{:S(2)}) collective-permute-start(bf16[2,2,128,256]{3,2,1,0:T(8,128)(2,1)S(1)} %get-tuple-element.90), channel_id=1, source_target_pairs={{6,0},{7,1},{0,2},{1,3},{2,4},{3,5},{4,6},{5,7},{14,8},{15,9},{8,1... | collective-permute-start | bytes 786440 | tf_op jit(solution)/shard_map/ppermute | solution.py:557
  42.2 3.0 %collective-permute-start.12 = (bf16[2,2,128,256]{3,2,1,0:T(8,128)(2,1)S(1)}, bf16[2,2,128,256]{3,2,1,0:T(8,128)(2,1)S(1)}, u32[]{:S(2)}, u32[]{:S(2)}) collective-permute-start(bf16[2,2,128,256]{3,2,1,0:T(8,128)(2,1)S(1)} %get-tuple-element.91), channel_id=1, source_target_pairs={{2,0},{3,1},{4,2},{5,3},{6,4},{7,5},{0,6},{1,7},{10,8},{11,9},{12,... | collective-permute-start | bytes 786440 | tf_op jit(solution)/shard_map/ppermute | solution.py:557
  45.1 1.8 %forward_own_near.1.keep = f32[24,128,256]{2,1,0:T(8,128)S(1)} custom-call(s32[1,640]{1,0:T(1,128)S(1)} %get-tuple-element.88.list_ref, s32[1,384]{1,0:T(1,128)S(1)} %get-tuple-element.78.tgt_ref, bf16[384,128,128]{2,1,0:T(8,128)(2,1)S(1)} %get-tuple-element.79.held, f32[64,128,256]{2,1,0:T(8,128)S(1)} %forward_early.1.early, ...), custom_call_target="tpu_custom_call" | custom-call | flops 1610612736 | bytes 12582912 | tf_op jit(solution)/shard_map/forward_own_near/pallas_call | solution.py:271
  47.0 4.6 %collective-permute-done.11.low = bf16[2,2,128,256]{3,2,1,0:T(8,128)(2,1)S(1)} collective-permute-done((bf16[2,2,128,256]{3,2,1,0:T(8,128)(2,1)S(1)}, bf16[2,2,128,256]{3,2,1,0:T(8,128)(2,1)S(1)}, u32[]{:S(2)}, u32[]{:S(2)}) %collective-permute-start.11) | collective-permute-done | bytes 262176 | tf_op jit(solution)/shard_map/ppermute | solution.py:557
  51.6 0.4 collective-permute-done.12.high
  52.1 0.4 relay_sums.1
  52.5 1.8 %collective-permute-start.13 = (bf16[4,128,256]{2,1,0:T(8,128)(2,1)S(1)}, bf16[4,128,256]{2,1,0:T(8,128)(2,1)S(1)}, u32[]{:S(2)}, u32[]{:S(2)}) collective-permute-start(bf16[4,128,256]{2,1,0:T(8,128)(2,1)S(1)} %get-tuple-element.95), channel_id=1, source_target_pairs={{6,0},{7,1},{0,2},{1,3},{2,4},{3,5},{4,6},{5,7},{14,8},{15,9},{8,1... | collective-permute-start | bytes 786440 | tf_op jit(solution)/shard_map/ppermute | solution.py:557
  54.3 1.5 %collective-permute-start.14 = (bf16[4,128,256]{2,1,0:T(8,128)(2,1)S(1)}, bf16[4,128,256]{2,1,0:T(8,128)(2,1)S(1)}, u32[]{:S(2)}, u32[]{:S(2)}) collective-permute-start(bf16[4,128,256]{2,1,0:T(8,128)(2,1)S(1)} %get-tuple-element.96), channel_id=1, source_target_pairs={{2,0},{3,1},{4,2},{5,3},{6,4},{7,5},{0,6},{1,7},{10,8},{11,9},{12,... | collective-permute-start | bytes 786440 | tf_op jit(solution)/shard_map/ppermute | solution.py:557
  55.8 5.5 %collective-permute-done.13 = bf16[4,128,256]{2,1,0:T(8,128)(2,1)S(1)} collective-permute-done((bf16[4,128,256]{2,1,0:T(8,128)(2,1)S(1)}, bf16[4,128,256]{2,1,0:T(8,128)(2,1)S(1)}, u32[]{:S(2)}, u32[]{:S(2)}) %collective-permute-start.13) | collective-permute-done | bytes 262176 | tf_op jit(solution)/shard_map/ppermute | solution.py:557
  61.4 0.8 collective-permute-start.15
  62.3 2.5 %collective-permute-start.16 = (bf16[4,128,256]{2,1,0:T(8,128)(2,1)S(1)}, bf16[4,128,256]{2,1,0:T(8,128)(2,1)S(1)}, u32[]{:S(2)}, u32[]{:S(2)}) collective-permute-start(bf16[4,128,256]{2,1,0:T(8,128)(2,1)S(1)} %get-tuple-element.98), channel_id=1, source_target_pairs={{2,0},{3,1},{4,2},{5,3},{6,4},{7,5},{0,6},{1,7},{10,8},{11,9},{12,... | collective-permute-start | bytes 786440 | tf_op jit(solution)/shard_map/ppermute | solution.py:557
  64.7 0.4 collective-permute-start.17
  65.2 4.1 %collective-permute-done.15.refs_1_ = bf16[4,128,256]{2,1,0:T(8,128)(2,1)S(1)} collective-permute-done((bf16[4,128,256]{2,1,0:T(8,128)(2,1)S(1)}, bf16[4,128,256]{2,1,0:T(8,128)(2,1)S(1)}, u32[]{:S(2)}, u32[]{:S(2)}) %collective-permute-start.15) | collective-permute-done | bytes 262176 | tf_op jit(solution)/shard_map/ppermute | solution.py:557
  69.3 1.8 %collective-permute-done.17.refs_3_ = bf16[4,128,256]{2,1,0:T(8,128)(2,1)S(1)} collective-permute-done((bf16[4,128,256]{2,1,0:T(8,128)(2,1)S(1)}, bf16[4,128,256]{2,1,0:T(8,128)(2,1)S(1)}, u32[]{:S(2)}, u32[]{:S(2)}) %collective-permute-start.17) | collective-permute-done | bytes 262176 | tf_op jit(solution)/shard_map/ppermute | solution.py:557
  71.1 1.5 %dense_layer.1 = (bf16[512,256]{1,0:T(8,128)(2,1)}, bf16[4,256,128]{2,1,0:T(8,128)(2,1)S(1)}, f32[264,256]{1,0:T(8,128)S(1)}) custom-call(f32[2,4,128,256]{3,2,1,0:T(8,128)S(1)} %get-tuple-element.92.refs_0_, bf16[4,128,256]{2,1,0:T(8,128)(2,1)S(1)} %collective-permute-done.15.refs_1_, bf16[4,128,256]{2,1,0:T(8,128)(2,1)S(1)} %collective-permute-done.16.refs_2_, ...), custom_call_target="tpu_custom_call" | custom-call | flops 201326592 | bytes 4194304 | tf_op jit(solution)/shard_map/dense_layer/pallas_call | solution.py:436
  72.6 0.6 collective-permute-start.18
  73.3 3.2 %collective-permute-start.20 = (bf16[4,256,128]{2,1,0:T(8,128)(2,1)S(1)}, bf16[4,256,128]{2,1,0:T(8,128)(2,1)S(1)}, u32[]{:S(2)}, u32[]{:S(2)}) collective-permute-start(bf16[4,256,128]{2,1,0:T(8,128)(2,1)S(1)} %get-tuple-element.102.refs_0_), channel_id=1, source_target_pairs={{2,0},{3,1},{4,2},{5,3},{6,4},{7,5},{0,6},{1,7},{10,8},{11,9},{12,... | collective-permute-start | bytes 786440 | tf_op jit(solution)/shard_map/ppermute | solution.py:557
  76.5 4.8 %collective-permute-done.18.refs_3_ = bf16[4,256,128]{2,1,0:T(8,128)(2,1)S(1)} collective-permute-done((bf16[4,256,128]{2,1,0:T(8,128)(2,1)S(1)}, bf16[4,256,128]{2,1,0:T(8,128)(2,1)S(1)}, u32[]{:S(2)}, u32[]{:S(2)}) %collective-permute-start.18) | collective-permute-done | bytes 262176 | tf_op jit(solution)/shard_map/ppermute | solution.py:557
  81.3 1.6 %collective-permute-done.22.refs_2_ = bf16[4,256,128]{2,1,0:T(8,128)(2,1)S(1)} collective-permute-done((bf16[4,256,128]{2,1,0:T(8,128)(2,1)S(1)}, bf16[4,256,128]{2,1,0:T(8,128)(2,1)S(1)}, u32[]{:S(2)}, u32[]{:S(2)}) %collective-permute-start.22) | collective-permute-done | bytes 262176 | tf_op jit(solution)/shard_map/ppermute | solution.py:557
  83.1 0.5 collective-permute-start.25
  83.8 3.2 %collective-permute-start.21 = (bf16[6,256,128]{2,1,0:T(8,128)(2,1)S(1)}, bf16[6,256,128]{2,1,0:T(8,128)(2,1)S(1)}, u32[]{:S(2)}, u32[]{:S(2)}) collective-permute-start(bf16[6,256,128]{2,1,0:T(8,128)(2,1)S(1)} %get-tuple-element.151), channel_id=1, source_target_pairs={{2,0},{3,1},{4,2},{5,3},{6,4},{7,5},{0,6},{1,7},{10,8},{11,9},{12,... | collective-permute-start | bytes 1179656 | tf_op jit(solution)/shard_map/ppermute | solution.py:557
  87.0 3.4 %backward_early.1.early = f32[32,256,128]{2,1,0:T(8,128)S(1)} custom-call(s32[1,640]{1,0:T(1,128)S(1)} %get-tuple-element.135.list_ref, s32[1,384]{1,0:T(1,128)S(1)} %get-tuple-element.106.tgt_ref, bf16[384,128,128]{2,1,0:T(8,128)(2,1)S(1)} %get-tuple-element.79.held, bf16[4,256,128]{2,1,0:T(8,128)(2,1)S(1)} %get-tuple-element.102.refs_0_, ...), custom_call_target="tpu_custom_call" | custom-call | flops 1610612736 | bytes 12582912 | tf_op jit(solution)/shard_map/backward_early/pallas_call | solution.py:242
  90.5 4.5 %collective-permute-done.24 = f32[264,256]{1,0:T(8,128)S(1)} collective-permute-done((f32[264,256]{1,0:T(8,128)S(1)}, f32[264,256]{1,0:T(8,128)S(1)}, u32[]{:S(2)}, u32[]{:S(2)}) %collective-permute-start.24) | collective-permute-done | bytes 270368 | tf_op jit(solution)/shard_map/ppermute | solution.py:623
  95.0 1.1 collective-permute-done.23.refs_1_
  96.3 1.2 collective-permute-start.29
  97.5 2.1 %collective-permute-start.28 = (bf16[2,256,128]{2,1,0:T(8,128)(2,1)S(1)}, bf16[2,256,128]{2,1,0:T(8,128)(2,1)S(1)}, u32[]{:S(2)}, u32[]{:S(2)}) collective-permute-start(bf16[2,256,128]{2,1,0:T(8,128)(2,1)S(1)} %slice.54), channel_id=1, source_target_pairs={{2,0},{3,1},{4,2},{5,3},{6,4},{7,5},{0,6},{1,7},{10,8},{11,9},{12,... | collective-permute-start | bytes 393224 | tf_op jit(solution)/shard_map/ppermute | solution.py:557
  99.7 1.4 collective-permute-start.27
  101.0 2.5 %collective-permute-done.29.refs_3_ = bf16[2,256,128]{2,1,0:T(8,128)(2,1)S(1)} collective-permute-done((bf16[2,256,128]{2,1,0:T(8,128)(2,1)S(1)}, bf16[2,256,128]{2,1,0:T(8,128)(2,1)S(1)}, u32[]{:S(2)}, u32[]{:S(2)}) %collective-permute-start.29) | collective-permute-done | bytes 131104 | tf_op jit(solution)/shard_map/ppermute | solution.py:557
  103.7 4.4 %collective-permute-done.27 = f32[264,256]{1,0:T(8,128)S(1)} collective-permute-done((f32[264,256]{1,0:T(8,128)S(1)}, f32[264,256]{1,0:T(8,128)S(1)}, u32[]{:S(2)}, u32[]{:S(2)}) %collective-permute-start.27) | collective-permute-done | bytes 270368 | tf_op jit(solution)/shard_map/ppermute | solution.py:623
  108.2 1.3 collective-permute-start.32
  109.5 3.5 %backward_across.1 = (f32[4,256,128]{2,1,0:T(8,128)S(1)}, bf16[4,256,128]{2,1,0:T(8,128)(2,1)S(1)}, bf16[4,256,128]{2,1,0:T(8,128)(2,1)S(1)}, bf16[2,256,128]{2,...) custom-call(s32[1,640]{1,0:T(1,128)S(1)} %get-tuple-element.135.list_ref, ...), custom_call_target="tpu_custom_call" | custom-call | flops 1610612736 | bytes 12582912 | tf_op jit(solution)/shard_map/backward_across/pallas_call | solution.py:271
  113.0 1.7 %collective-permute-done.32 = bf16[264,256]{1,0:T(8,128)(2,1)S(1)} collective-permute-done((bf16[264,256]{1,0:T(8,128)(2,1)S(1)}, bf16[264,256]{1,0:T(8,128)(2,1)S(1)}, u32[]{:S(2)}, u32[]{:S(2)}) %collective-permute-start.32) | collective-permute-done | bytes 135200 | tf_op jit(solution)/shard_map/ppermute | solution.py:623
  114.8 1.2 collective-permute-start.34
  116.0 2.1 %collective-permute-start.35 = (bf16[2,256,128]{2,1,0:T(8,128)(2,1)S(1)}, bf16[2,256,128]{2,1,0:T(8,128)(2,1)S(1)}, u32[]{:S(2)}, u32[]{:S(2)}) collective-permute-start(bf16[2,256,128]{2,1,0:T(8,128)(2,1)S(1)} %get-tuple-element.127), channel_id=1, source_target_pairs={{16,0},{32,16},{48,32},{0,48},{80,64},{96,80},{112,96},{64,112},{1... | collective-permute-start | bytes 393224 | tf_op jit(solution)/shard_map/ppermute | solution.py:549
  118.1 1.3 collective-permute-start.33
  119.4 1.6 %backward_far_own.1 = (bf16[2,256,128]{2,1,0:T(8,128)(2,1)S(1)}, bf16[2,256,128]{2,1,0:T(8,128)(2,1)S(1)}, f32[4,256,128]{2,1,0:T(8,128)S(1)}) custom-call(s32[1,640]{1,0:T(1,128)S(1)} %get-tuple-element.135.list_ref, s32[1,384]{1,0:T(1,128)S(1)} %get-tuple-element.106.tgt_ref, bf16[384,128,128]{2,1,0:T(8,128)(2,1)S(1)} %get-tuple-element.79.held, ...), custom_call_target="tpu_custom_call" | custom-call | flops 1610612736 | bytes 12582912 | tf_op jit(solution)/shard_map/backward_far_own/pallas_call | solution.py:271
  121.2 3.5 %collective-permute-done.33 = bf16[264,256]{1,0:T(8,128)(2,1)S(1)} collective-permute-done((bf16[264,256]{1,0:T(8,128)(2,1)S(1)}, bf16[264,256]{1,0:T(8,128)(2,1)S(1)}, u32[]{:S(2)}, u32[]{:S(2)}) %collective-permute-start.33) | collective-permute-done | bytes 135200 | tf_op jit(solution)/shard_map/ppermute | solution.py:623
  124.6 3.2 %collective-permute-start.37 = (bf16[6,256,128]{2,1,0:T(8,128)(2,1)S(1)}, bf16[6,256,128]{2,1,0:T(8,128)(2,1)S(1)}, u32[]{:S(2)}, u32[]{:S(2)}) collective-permute-start(bf16[6,256,128]{2,1,0:T(8,128)(2,1)S(1)} %get-tuple-element.133), channel_id=1, source_target_pairs={{16,0},{32,16},{48,32},{0,48},{80,64},{96,80},{112,96},{64,112},{1... | collective-permute-start | bytes 1179656 | tf_op jit(solution)/shard_map/ppermute | solution.py:549
  128.0 1.6 %backward_near.1 = (bf16[4,256,128]{2,1,0:T(8,128)(2,1)S(1)}, bf16[4,256,128]{2,1,0:T(8,128)(2,1)S(1)}) custom-call(s32[1,640]{1,0:T(1,128)S(1)} %get-tuple-element.135.list_ref, s32[1,384]{1,0:T(1,128)S(1)} %get-tuple-element.106.tgt_ref, bf16[384,128,128]{2,1,0:T(8,128)(2,1)S(1)} %get-tuple-element.79.held, f32[32,256,128]{2,1,0:T(8,128)S(1)} %backward_early.1.early, ...), custom_call_target="tpu_custom_call" | custom-call | flops 1610612736 | bytes 12582912 | tf_op jit(solution)/shard_map/backward_near/pallas_call | solution.py:271
  129.6 3.4 %collective-permute-done.38 = bf16[264,256]{1,0:T(8,128)(2,1)S(1)} collective-permute-done((bf16[264,256]{1,0:T(8,128)(2,1)S(1)}, bf16[264,256]{1,0:T(8,128)(2,1)S(1)}, u32[]{:S(2)}, u32[]{:S(2)}) %collective-permute-start.38) | collective-permute-done | bytes 135200 | tf_op jit(solution)/shard_map/ppermute | solution.py:623
  133.0 0.6 collective-permute-done.36
  133.7 1.5 %collective-permute-start.39 = (bf16[4,256,128]{2,1,0:T(8,128)(2,1)S(1)}, bf16[4,256,128]{2,1,0:T(8,128)(2,1)S(1)}, u32[]{:S(2)}, u32[]{:S(2)}) collective-permute-start(bf16[4,256,128]{2,1,0:T(8,128)(2,1)S(1)} %add_convert_fusion.1), channel_id=1, source_target_pairs={{64,0},{80,16},{96,32},{112,48},{0,64},{16,80},{32,96},{48,112},{6... | collective-permute-start | bytes 786440 | tf_op jit(solution)/shard_map/ppermute | solution.py:549
  135.3 1.5 %collective-permute-start.42 = (bf16[264,256]{1,0:T(8,128)(2,1)S(1)}, bf16[264,256]{1,0:T(8,128)(2,1)S(1)}, u32[]{:S(2)}, u32[]{:S(2)}) collective-permute-start(bf16[264,256]{1,0:T(8,128)(2,1)S(1)} %add_convert_fusion.2.mine), channel_id=1, source_target_pairs={{4,0},{5,1},{6,2},{7,3},{0,4},{1,5},{2,6},{3,7},{12,8},{13,9},{14,... | collective-permute-start | bytes 405512 | tf_op jit(solution)/shard_map/ppermute | solution.py:623
  137.2 3.0 %collective-permute-start.41 = (bf16[4,256,128]{2,1,0:T(8,128)(2,1)S(1)}, bf16[4,256,128]{2,1,0:T(8,128)(2,1)S(1)}, u32[]{:S(2)}, u32[]{:S(2)}) collective-permute-start(bf16[4,256,128]{2,1,0:T(8,128)(2,1)S(1)} %get-tuple-element.143), channel_id=1, source_target_pairs={{16,0},{32,16},{48,32},{0,48},{80,64},{96,80},{112,96},{64,112},{1... | collective-permute-start | bytes 786440 | tf_op jit(solution)/shard_map/ppermute | solution.py:549
  140.2 1.4 collective-permute-done.39.across
  141.9 2.6 %collective-permute-done.40.up = bf16[4,256,128]{2,1,0:T(8,128)(2,1)S(1)} collective-permute-done((bf16[4,256,128]{2,1,0:T(8,128)(2,1)S(1)}, bf16[4,256,128]{2,1,0:T(8,128)(2,1)S(1)}, u32[]{:S(2)}, u32[]{:S(2)}) %collective-permute-start.40) | collective-permute-done | bytes 262176 | tf_op jit(solution)/shard_map/ppermute | solution.py:549
  144.5 0.9 finish_grads.1
  (70 shorter events, 2.5 us)
Async XLA Ops:
  0.6 13.2 %collective-permute-start.2 = (bf16[4,128,256]{2,1,0:T(8,128)(2,1)}, bf16[4,128,256]{2,1,0:T(8,128)(2,1)S(1)}, u32[]{:S(2)}, u32[]{:S(2)}) collective-permute-start(bf16[4,128,256]{2,1,0:T(8,128)(2,1)} %bitcast.21), channel_id=1, source_target_pairs={{64,0},{80,16},{96,32},{112,48},{0,64},{16,80},{32,96},{48,112},{6... | collective-permute-start | bytes 786440 | tf_op jit(solution)/shard_map/ppermute | solution.py:549
  4.0 10.3 %collective-permute-start.1 = (bf16[4,128,256]{2,1,0:T(8,128)(2,1)}, bf16[4,128,256]{2,1,0:T(8,128)(2,1)S(1)}, u32[]{:S(2)}, u32[]{:S(2)}) collective-permute-start(bf16[4,128,256]{2,1,0:T(8,128)(2,1)} %bitcast.22), channel_id=1, source_target_pairs={{48,0},{0,16},{16,32},{32,48},{112,64},{64,80},{80,96},{96,112},{4... | collective-permute-start | bytes 786440 | tf_op jit(solution)/shard_map/ppermute | solution.py:549
  5.9 8.4 %collective-permute-start = (bf16[4,128,256]{2,1,0:T(8,128)(2,1)}, bf16[4,128,256]{2,1,0:T(8,128)(2,1)S(1)}, u32[]{:S(2)}, u32[]{:S(2)}) collective-permute-start(bf16[4,128,256]{2,1,0:T(8,128)(2,1)} %bitcast.23), channel_id=1, source_target_pairs={{16,0},{32,16},{48,32},{0,48},{80,64},{96,80},{112,96},{64,112},{1... | collective-permute-start | bytes 786440 | tf_op jit(solution)/shard_map/ppermute | solution.py:549
  9.4 11.5 %copy-start = (bf16[512,256]{1,0:T(8,128)(2,1)S(1)}, bf16[512,256]{1,0:T(8,128)(2,1)}, u32[]{:S(2)}) copy-start(bf16[512,256]{1,0:T(8,128)(2,1)} %param.8) | copy-start | bytes 786436
  14.3 9.8 %collective-permute-start.4 = (bf16[4,128,256]{2,1,0:T(8,128)(2,1)S(1)}, bf16[4,128,256]{2,1,0:T(8,128)(2,1)S(1)}, u32[]{:S(2)}, u32[]{:S(2)}) collective-permute-start(bf16[4,128,256]{2,1,0:T(8,128)(2,1)S(1)} %collective-permute-done.2.refs_2_), channel_id=1, source_target_pairs={{48,0},{0,16},{16,32},{32,48},{112,64},{64,80},{80,96},{96,112},{4... | collective-permute-start | bytes 786440 | tf_op jit(solution)/shard_map/ppermute | solution.py:549
  15.5 8.6 %collective-permute-start.3 = (bf16[4,128,256]{2,1,0:T(8,128)(2,1)S(1)}, bf16[4,128,256]{2,1,0:T(8,128)(2,1)S(1)}, u32[]{:S(2)}, u32[]{:S(2)}) collective-permute-start(bf16[4,128,256]{2,1,0:T(8,128)(2,1)S(1)} %collective-permute-done.2.refs_2_), channel_id=1, source_target_pairs={{16,0},{32,16},{48,32},{0,48},{80,64},{96,80},{112,96},{64,112},{1... | collective-permute-start | bytes 786440 | tf_op jit(solution)/shard_map/ppermute | solution.py:549
  17.6 9.9 %collective-permute-start.6 = (bf16[2,128,256]{2,1,0:T(8,128)(2,1)S(1)}, bf16[2,128,256]{2,1,0:T(8,128)(2,1)S(1)}, u32[]{:S(2)}, u32[]{:S(2)}) collective-permute-start(bf16[2,128,256]{2,1,0:T(8,128)(2,1)S(1)} %slice.46), channel_id=1, source_target_pairs={{48,0},{0,16},{16,32},{32,48},{112,64},{64,80},{80,96},{96,112},{4... | collective-permute-start | bytes 393224 | tf_op jit(solution)/shard_map/ppermute | solution.py:549
  17.6 9.8 %collective-permute-start.5 = (bf16[2,128,256]{2,1,0:T(8,128)(2,1)S(1)}, bf16[2,128,256]{2,1,0:T(8,128)(2,1)S(1)}, u32[]{:S(2)}, u32[]{:S(2)}) collective-permute-start(bf16[2,128,256]{2,1,0:T(8,128)(2,1)S(1)} %slice.45), channel_id=1, source_target_pairs={{16,0},{32,16},{48,32},{0,48},{80,64},{96,80},{112,96},{64,112},{1... | collective-permute-start | bytes 393224 | tf_op jit(solution)/shard_map/ppermute | solution.py:549
  24.1 6.2 %collective-permute-start.8 = (bf16[2,128,256]{2,1,0:T(8,128)(2,1)S(1)}, bf16[2,128,256]{2,1,0:T(8,128)(2,1)S(1)}, u32[]{:S(2)}, u32[]{:S(2)}) collective-permute-start(bf16[2,128,256]{2,1,0:T(8,128)(2,1)S(1)} %slice.48), channel_id=1, source_target_pairs={{48,0},{0,16},{16,32},{32,48},{112,64},{64,80},{80,96},{96,112},{4... | collective-permute-start | bytes 393224 | tf_op jit(solution)/shard_map/ppermute | solution.py:549
  25.3 5.1 %collective-permute-start.7 = (bf16[2,128,256]{2,1,0:T(8,128)(2,1)S(1)}, bf16[2,128,256]{2,1,0:T(8,128)(2,1)S(1)}, u32[]{:S(2)}, u32[]{:S(2)}) collective-permute-start(bf16[2,128,256]{2,1,0:T(8,128)(2,1)S(1)} %slice.47), channel_id=1, source_target_pairs={{16,0},{32,16},{48,32},{0,48},{80,64},{96,80},{112,96},{64,112},{1... | collective-permute-start | bytes 393224 | tf_op jit(solution)/shard_map/ppermute | solution.py:549
  33.8 18.3 %collective-permute-start.10 = (bf16[2,3,4,128,256]{4,3,2,1,0:T(8,128)(2,1)S(1)}, bf16[2,3,4,128,256]{4,3,2,1,0:T(8,128)(2,1)S(1)}, u32[]{:S(2)}, u32[]{:S(2)}) collective-permute-start(bf16[2,3,4,128,256]{4,3,2,1,0:T(8,128)(2,1)S(1)} %get-tuple-element.89), channel_id=1, source_target_pairs={{1,0},{0,1},{3,2},{2,3},{5,4},{4,5},{7,6},{6,7},{9,8},{8,9},{11,10... | collective-permute-start | bytes 4718600 | tf_op jit(solution)/shard_map/ppermute | solution.py:557
  33.8 4.1 %collective-permute-start.9 = (bf16[2,4,128,256]{3,2,1,0:T(8,128)(2,1)S(1)}, bf16[2,4,128,256]{3,2,1,0:T(8,128)(2,1)S(1)}, u32[]{:S(2)}, u32[]{:S(2)}) collective-permute-start(bf16[2,4,128,256]{3,2,1,0:T(8,128)(2,1)S(1)} %get-tuple-element.87), channel_id=1, source_target_pairs={{1,0},{0,1},{3,2},{2,3},{5,4},{4,5},{7,6},{6,7},{9,8},{8,9},{11,10... | collective-permute-start | bytes 1572872 | tf_op jit(solution)/shard_map/ppermute | solution.py:557
  38.2 13.4 %collective-permute-start.11 = (bf16[2,2,128,256]{3,2,1,0:T(8,128)(2,1)S(1)}, bf16[2,2,128,256]{3,2,1,0:T(8,128)(2,1)S(1)}, u32[]{:S(2)}, u32[]{:S(2)}) collective-permute-start(bf16[2,2,128,256]{3,2,1,0:T(8,128)(2,1)S(1)} %get-tuple-element.90), channel_id=1, source_target_pairs={{6,0},{7,1},{0,2},{1,3},{2,4},{3,5},{4,6},{5,7},{14,8},{15,9},{8,1... | collective-permute-start | bytes 786440 | tf_op jit(solution)/shard_map/ppermute | solution.py:557
  42.2 9.9 %collective-permute-start.12 = (bf16[2,2,128,256]{3,2,1,0:T(8,128)(2,1)S(1)}, bf16[2,2,128,256]{3,2,1,0:T(8,128)(2,1)S(1)}, u32[]{:S(2)}, u32[]{:S(2)}) collective-permute-start(bf16[2,2,128,256]{3,2,1,0:T(8,128)(2,1)S(1)} %get-tuple-element.91), channel_id=1, source_target_pairs={{2,0},{3,1},{4,2},{5,3},{6,4},{7,5},{0,6},{1,7},{10,8},{11,9},{12,... | collective-permute-start | bytes 786440 | tf_op jit(solution)/shard_map/ppermute | solution.py:557
  47.0 24.1 %copy-start.1 = (bf16[512,256]{1,0:T(8,128)(2,1)S(1)}, bf16[512,256]{1,0:T(8,128)(2,1)}, u32[]{:S(2)}) copy-start(bf16[512,256]{1,0:T(8,128)(2,1)} %refs_6_.1) | copy-start | bytes 786436
  47.0 24.1 %copy-start.2 = (bf16[256,256]{1,0:T(8,128)(2,1)S(1)}, bf16[256,256]{1,0:T(8,128)(2,1)}, u32[]{:S(2)}) copy-start(bf16[256,256]{1,0:T(8,128)(2,1)} %refs_4_.1) | copy-start | bytes 393220
  47.0 24.1 %copy-start.3 = (f32[256]{0:T(256)S(1)}, f32[256]{0:T(256)}, u32[]{:S(2)}) copy-start(f32[256]{0:T(256)} %param.10) | copy-start | bytes 3076
  52.5 8.8 %collective-permute-start.13 = (bf16[4,128,256]{2,1,0:T(8,128)(2,1)S(1)}, bf16[4,128,256]{2,1,0:T(8,128)(2,1)S(1)}, u32[]{:S(2)}, u32[]{:S(2)}) collective-permute-start(bf16[4,128,256]{2,1,0:T(8,128)(2,1)S(1)} %get-tuple-element.95), channel_id=1, source_target_pairs={{6,0},{7,1},{0,2},{1,3},{2,4},{3,5},{4,6},{5,7},{14,8},{15,9},{8,1... | collective-permute-start | bytes 786440 | tf_op jit(solution)/shard_map/ppermute | solution.py:557
  54.3 7.0 %collective-permute-start.14 = (bf16[4,128,256]{2,1,0:T(8,128)(2,1)S(1)}, bf16[4,128,256]{2,1,0:T(8,128)(2,1)S(1)}, u32[]{:S(2)}, u32[]{:S(2)}) collective-permute-start(bf16[4,128,256]{2,1,0:T(8,128)(2,1)S(1)} %get-tuple-element.96), channel_id=1, source_target_pairs={{2,0},{3,1},{4,2},{5,3},{6,4},{7,5},{0,6},{1,7},{10,8},{11,9},{12,... | collective-permute-start | bytes 786440 | tf_op jit(solution)/shard_map/ppermute | solution.py:557
  61.4 7.9 %collective-permute-start.15 = (bf16[4,128,256]{2,1,0:T(8,128)(2,1)S(1)}, bf16[4,128,256]{2,1,0:T(8,128)(2,1)S(1)}, u32[]{:S(2)}, u32[]{:S(2)}) collective-permute-start(bf16[4,128,256]{2,1,0:T(8,128)(2,1)S(1)} %get-tuple-element.97), channel_id=1, source_target_pairs={{6,0},{7,1},{0,2},{1,3},{2,4},{3,5},{4,6},{5,7},{14,8},{15,9},{8,1... | collective-permute-start | bytes 786440 | tf_op jit(solution)/shard_map/ppermute | solution.py:557
  62.3 7.0 %collective-permute-start.16 = (bf16[4,128,256]{2,1,0:T(8,128)(2,1)S(1)}, bf16[4,128,256]{2,1,0:T(8,128)(2,1)S(1)}, u32[]{:S(2)}, u32[]{:S(2)}) collective-permute-start(bf16[4,128,256]{2,1,0:T(8,128)(2,1)S(1)} %get-tuple-element.98), channel_id=1, source_target_pairs={{2,0},{3,1},{4,2},{5,3},{6,4},{7,5},{0,6},{1,7},{10,8},{11,9},{12,... | collective-permute-start | bytes 786440 | tf_op jit(solution)/shard_map/ppermute | solution.py:557
  64.7 6.4 %collective-permute-start.17 = (bf16[4,128,256]{2,1,0:T(8,128)(2,1)S(1)}, bf16[4,128,256]{2,1,0:T(8,128)(2,1)S(1)}, u32[]{:S(2)}, u32[]{:S(2)}) collective-permute-start(bf16[4,128,256]{2,1,0:T(8,128)(2,1)S(1)} %fusion.1), channel_id=1, source_target_pairs={{8,0},{9,1},{10,2},{11,3},{12,4},{13,5},{14,6},{15,7},{0,8},{1,9},... | collective-permute-start | bytes 786440 | tf_op jit(solution)/shard_map/ppermute | solution.py:557
  72.6 3.9 %collective-permute-start.19 = (f32[264,256]{1,0:T(8,128)S(1)}, f32[264,256]{1,0:T(8,128)S(1)}, u32[]{:S(2)}, u32[]{:S(2)}) collective-permute-start(f32[264,256]{1,0:T(8,128)S(1)} %get-tuple-element.103), channel_id=1, source_target_pairs={{1,0},{0,1},{3,2},{2,3},{5,4},{4,5},{7,6},{6,7},{9,8},{8,9},{11,10... | collective-permute-start | bytes 811016 | tf_op jit(solution)/shard_map/ppermute | solution.py:623
  72.6 8.7 %collective-permute-start.18 = (bf16[4,256,128]{2,1,0:T(8,128)(2,1)S(1)}, bf16[4,256,128]{2,1,0:T(8,128)(2,1)S(1)}, u32[]{:S(2)}, u32[]{:S(2)}) collective-permute-start(bf16[4,256,128]{2,1,0:T(8,128)(2,1)S(1)} %get-tuple-element.102.refs_0_), channel_id=1, source_target_pairs={{8,0},{9,1},{10,2},{11,3},{12,4},{13,5},{14,6},{15,7},{0,8},{1,9},... | collective-permute-start | bytes 786440 | tf_op jit(solution)/shard_map/ppermute | solution.py:557
  73.3 9.6 %collective-permute-start.22 = (bf16[4,256,128]{2,1,0:T(8,128)(2,1)S(1)}, bf16[4,256,128]{2,1,0:T(8,128)(2,1)S(1)}, u32[]{:S(2)}, u32[]{:S(2)}) collective-permute-start(bf16[4,256,128]{2,1,0:T(8,128)(2,1)S(1)} %get-tuple-element.102.refs_0_), channel_id=1, source_target_pairs={{6,0},{7,1},{0,2},{1,3},{2,4},{3,5},{4,6},{5,7},{14,8},{15,9},{8,1... | collective-permute-start | bytes 786440 | tf_op jit(solution)/shard_map/ppermute | solution.py:557
  73.3 9.6 %collective-permute-start.20 = (bf16[4,256,128]{2,1,0:T(8,128)(2,1)S(1)}, bf16[4,256,128]{2,1,0:T(8,128)(2,1)S(1)}, u32[]{:S(2)}, u32[]{:S(2)}) collective-permute-start(bf16[4,256,128]{2,1,0:T(8,128)(2,1)S(1)} %get-tuple-element.102.refs_0_), channel_id=1, source_target_pairs={{2,0},{3,1},{4,2},{5,3},{6,4},{7,5},{0,6},{1,7},{10,8},{11,9},{12,... | collective-permute-start | bytes 786440 | tf_op jit(solution)/shard_map/ppermute | solution.py:557
  83.0 4.0 %collective-permute-start.26 = (bf16[12,256,128]{2,1,0:T(8,128)(2,1)S(1)}, bf16[12,256,128]{2,1,0:T(8,128)(2,1)S(1)}, u32[]{:S(2)}, u32[]{:S(2)}) collective-permute-start(bf16[12,256,128]{2,1,0:T(8,128)(2,1)S(1)} %pad_maximum_fusion), channel_id=1, source_target_pairs={{1,0},{0,1},{3,2},{2,3},{5,4},{4,5},{7,6},{6,7},{9,8},{8,9},{11,10... | collective-permute-start | bytes 2359304 | tf_op jit(solution)/shard_map/ppermute | solution.py:557
  83.1 3.9 %collective-permute-start.25 = (bf16[4,256,128]{2,1,0:T(8,128)(2,1)S(1)}, bf16[4,256,128]{2,1,0:T(8,128)(2,1)S(1)}, u32[]{:S(2)}, u32[]{:S(2)}) collective-permute-start(bf16[4,256,128]{2,1,0:T(8,128)(2,1)S(1)} %get-tuple-element.102.refs_0_), channel_id=1, source_target_pairs={{1,0},{0,1},{3,2},{2,3},{5,4},{4,5},{7,6},{6,7},{9,8},{8,9},{11,10... | collective-permute-start | bytes 786440 | tf_op jit(solution)/shard_map/ppermute | solution.py:557
  83.7 12.4 %collective-permute-start.23 = (bf16[6,256,128]{2,1,0:T(8,128)(2,1)S(1)}, bf16[6,256,128]{2,1,0:T(8,128)(2,1)S(1)}, u32[]{:S(2)}, u32[]{:S(2)}) collective-permute-start(bf16[6,256,128]{2,1,0:T(8,128)(2,1)S(1)} %get-tuple-element.150), channel_id=1, source_target_pairs={{6,0},{7,1},{0,2},{1,3},{2,4},{3,5},{4,6},{5,7},{14,8},{15,9},{8,1... | collective-permute-start | bytes 1179656 | tf_op jit(solution)/shard_map/ppermute | solution.py:557
  83.8 12.3 %collective-permute-start.21 = (bf16[6,256,128]{2,1,0:T(8,128)(2,1)S(1)}, bf16[6,256,128]{2,1,0:T(8,128)(2,1)S(1)}, u32[]{:S(2)}, u32[]{:S(2)}) collective-permute-start(bf16[6,256,128]{2,1,0:T(8,128)(2,1)S(1)} %get-tuple-element.151), channel_id=1, source_target_pairs={{2,0},{3,1},{4,2},{5,3},{6,4},{7,5},{0,6},{1,7},{10,8},{11,9},{12,... | collective-permute-start | bytes 1179656 | tf_op jit(solution)/shard_map/ppermute | solution.py:557
  87.0 8.0 %collective-permute-start.24 = (f32[264,256]{1,0:T(8,128)S(1)}, f32[264,256]{1,0:T(8,128)S(1)}, u32[]{:S(2)}, u32[]{:S(2)}) collective-permute-start(f32[264,256]{1,0:T(8,128)S(1)} %add.36), channel_id=1, source_target_pairs={{16,0},{0,16},{48,32},{32,48},{80,64},{64,80},{112,96},{96,112},{1... | collective-permute-start | bytes 811016 | tf_op jit(solution)/shard_map/ppermute | solution.py:623
  96.2 13.3 %collective-permute-start.30 = (bf16[12,256,128]{2,1,0:T(8,128)(2,1)S(1)}, bf16[12,256,128]{2,1,0:T(8,128)(2,1)S(1)}, u32[]{:S(2)}, u32[]{:S(2)}) collective-permute-start(bf16[12,256,128]{2,1,0:T(8,128)(2,1)S(1)} %pad_maximum_fusion.1), channel_id=1, source_target_pairs={{1,0},{0,1},{3,2},{2,3},{5,4},{4,5},{7,6},{6,7},{9,8},{8,9},{11,10... | collective-permute-start | bytes 2359304 | tf_op jit(solution)/shard_map/ppermute | solution.py:557
  96.3 7.3 %collective-permute-start.29 = (bf16[2,256,128]{2,1,0:T(8,128)(2,1)S(1)}, bf16[2,256,128]{2,1,0:T(8,128)(2,1)S(1)}, u32[]{:S(2)}, u32[]{:S(2)}) collective-permute-start(bf16[2,256,128]{2,1,0:T(8,128)(2,1)S(1)} %slice.55), channel_id=1, source_target_pairs={{6,0},{7,1},{0,2},{1,3},{2,4},{3,5},{4,6},{5,7},{14,8},{15,9},{8,1... | collective-permute-start | bytes 393224 | tf_op jit(solution)/shard_map/ppermute | solution.py:557
  97.5 6.1 %collective-permute-start.28 = (bf16[2,256,128]{2,1,0:T(8,128)(2,1)S(1)}, bf16[2,256,128]{2,1,0:T(8,128)(2,1)S(1)}, u32[]{:S(2)}, u32[]{:S(2)}) collective-permute-start(bf16[2,256,128]{2,1,0:T(8,128)(2,1)S(1)} %slice.54), channel_id=1, source_target_pairs={{2,0},{3,1},{4,2},{5,3},{6,4},{7,5},{0,6},{1,7},{10,8},{11,9},{12,... | collective-permute-start | bytes 393224 | tf_op jit(solution)/shard_map/ppermute | solution.py:557
  99.7 8.5 %collective-permute-start.27 = (f32[264,256]{1,0:T(8,128)S(1)}, f32[264,256]{1,0:T(8,128)S(1)}, u32[]{:S(2)}, u32[]{:S(2)}) collective-permute-start(f32[264,256]{1,0:T(8,128)S(1)} %add.37), channel_id=1, source_target_pairs={{8,0},{9,1},{10,2},{11,3},{12,4},{13,5},{14,6},{15,7},{0,8},{1,9},... | collective-permute-start | bytes 811016 | tf_op jit(solution)/shard_map/ppermute | solution.py:623
  103.6 5.9 %collective-permute-start.31 = (bf16[4,256,128]{2,1,0:T(8,128)(2,1)S(1)}, bf16[4,256,128]{2,1,0:T(8,128)(2,1)S(1)}, u32[]{:S(2)}, u32[]{:S(2)}) collective-permute-start(bf16[4,256,128]{2,1,0:T(8,128)(2,1)S(1)} %pad_maximum_fusion.4), channel_id=1, source_target_pairs={{1,0},{0,1},{3,2},{2,3},{5,4},{4,5},{7,6},{6,7},{9,8},{8,9},{11,10... | collective-permute-start | bytes 786440 | tf_op jit(solution)/shard_map/ppermute | solution.py:557
  108.2 6.6 %collective-permute-start.32 = (bf16[264,256]{1,0:T(8,128)(2,1)S(1)}, bf16[264,256]{1,0:T(8,128)(2,1)S(1)}, u32[]{:S(2)}, u32[]{:S(2)}) collective-permute-start(bf16[264,256]{1,0:T(8,128)(2,1)S(1)} %add.38), channel_id=1, source_target_pairs={{32,0},{48,16},{0,32},{16,48},{96,64},{112,80},{64,96},{80,112},{3... | collective-permute-start | bytes 405512 | tf_op jit(solution)/shard_map/ppermute | solution.py:623
  114.8 6.3 %collective-permute-start.34 = (bf16[2,256,128]{2,1,0:T(8,128)(2,1)S(1)}, bf16[2,256,128]{2,1,0:T(8,128)(2,1)S(1)}, u32[]{:S(2)}, u32[]{:S(2)}) collective-permute-start(bf16[2,256,128]{2,1,0:T(8,128)(2,1)S(1)} %get-tuple-element.126), channel_id=1, source_target_pairs={{48,0},{0,16},{16,32},{32,48},{112,64},{64,80},{80,96},{96,112},{4... | collective-permute-start | bytes 393224 | tf_op jit(solution)/shard_map/ppermute | solution.py:549
  116.0 5.1 %collective-permute-start.35 = (bf16[2,256,128]{2,1,0:T(8,128)(2,1)S(1)}, bf16[2,256,128]{2,1,0:T(8,128)(2,1)S(1)}, u32[]{:S(2)}, u32[]{:S(2)}) collective-permute-start(bf16[2,256,128]{2,1,0:T(8,128)(2,1)S(1)} %get-tuple-element.127), channel_id=1, source_target_pairs={{16,0},{32,16},{48,32},{0,48},{80,64},{96,80},{112,96},{64,112},{1... | collective-permute-start | bytes 393224 | tf_op jit(solution)/shard_map/ppermute | solution.py:549
  118.1 6.5 %collective-permute-start.33 = (bf16[264,256]{1,0:T(8,128)(2,1)S(1)}, bf16[264,256]{1,0:T(8,128)(2,1)S(1)}, u32[]{:S(2)}, u32[]{:S(2)}) collective-permute-start(bf16[264,256]{1,0:T(8,128)(2,1)S(1)} %add_convert_fusion.3), channel_id=1, source_target_pairs={{64,0},{80,16},{96,32},{112,48},{0,64},{16,80},{32,96},{48,112},{6... | collective-permute-start | bytes 405512 | tf_op jit(solution)/shard_map/ppermute | solution.py:623
  124.6 9.0 %collective-permute-start.36 = (bf16[6,256,128]{2,1,0:T(8,128)(2,1)S(1)}, bf16[6,256,128]{2,1,0:T(8,128)(2,1)S(1)}, u32[]{:S(2)}, u32[]{:S(2)}) collective-permute-start(bf16[6,256,128]{2,1,0:T(8,128)(2,1)S(1)} %get-tuple-element.132), channel_id=1, source_target_pairs={{48,0},{0,16},{16,32},{32,48},{112,64},{64,80},{80,96},{96,112},{4... | collective-permute-start | bytes 1179656 | tf_op jit(solution)/shard_map/ppermute | solution.py:549
  124.6 9.0 %collective-permute-start.37 = (bf16[6,256,128]{2,1,0:T(8,128)(2,1)S(1)}, bf16[6,256,128]{2,1,0:T(8,128)(2,1)S(1)}, u32[]{:S(2)}, u32[]{:S(2)}) collective-permute-start(bf16[6,256,128]{2,1,0:T(8,128)(2,1)S(1)} %get-tuple-element.133), channel_id=1, source_target_pairs={{16,0},{32,16},{48,32},{0,48},{80,64},{96,80},{112,96},{64,112},{1... | collective-permute-start | bytes 1179656 | tf_op jit(solution)/shard_map/ppermute | solution.py:549
  127.9 5.1 %collective-permute-start.38 = (bf16[264,256]{1,0:T(8,128)(2,1)S(1)}, bf16[264,256]{1,0:T(8,128)(2,1)S(1)}, u32[]{:S(2)}, u32[]{:S(2)}) collective-permute-start(bf16[264,256]{1,0:T(8,128)(2,1)S(1)} %convert_add_fusion), channel_id=1, source_target_pairs={{2,0},{3,1},{0,2},{1,3},{6,4},{7,5},{4,6},{5,7},{10,8},{11,9},{8,1... | collective-permute-start | bytes 405512 | tf_op jit(solution)/shard_map/ppermute | solution.py:623
  133.7 8.0 %collective-permute-start.39 = (bf16[4,256,128]{2,1,0:T(8,128)(2,1)S(1)}, bf16[4,256,128]{2,1,0:T(8,128)(2,1)S(1)}, u32[]{:S(2)}, u32[]{:S(2)}) collective-permute-start(bf16[4,256,128]{2,1,0:T(8,128)(2,1)S(1)} %add_convert_fusion.1), channel_id=1, source_target_pairs={{64,0},{80,16},{96,32},{112,48},{0,64},{16,80},{32,96},{48,112},{6... | collective-permute-start | bytes 786440 | tf_op jit(solution)/shard_map/ppermute | solution.py:549
  135.3 6.6 %collective-permute-start.42 = (bf16[264,256]{1,0:T(8,128)(2,1)S(1)}, bf16[264,256]{1,0:T(8,128)(2,1)S(1)}, u32[]{:S(2)}, u32[]{:S(2)}) collective-permute-start(bf16[264,256]{1,0:T(8,128)(2,1)S(1)} %add_convert_fusion.2.mine), channel_id=1, source_target_pairs={{4,0},{5,1},{6,2},{7,3},{0,4},{1,5},{2,6},{3,7},{12,8},{13,9},{14,... | collective-permute-start | bytes 405512 | tf_op jit(solution)/shard_map/ppermute | solution.py:623
  136.9 7.7 %collective-permute-start.40 = (bf16[4,256,128]{2,1,0:T(8,128)(2,1)S(1)}, bf16[4,256,128]{2,1,0:T(8,128)(2,1)S(1)}, u32[]{:S(2)}, u32[]{:S(2)}) collective-permute-start(bf16[4,256,128]{2,1,0:T(8,128)(2,1)S(1)} %get-tuple-element.142), channel_id=1, source_target_pairs={{48,0},{0,16},{16,32},{32,48},{112,64},{64,80},{80,96},{96,112},{4... | collective-permute-start | bytes 786440 | tf_op jit(solution)/shard_map/ppermute | solution.py:549
  137.2 7.3 %collective-permute-start.41 = (bf16[4,256,128]{2,1,0:T(8,128)(2,1)S(1)}, bf16[4,256,128]{2,1,0:T(8,128)(2,1)S(1)}, u32[]{:S(2)}, u32[]{:S(2)}) collective-permute-start(bf16[4,256,128]{2,1,0:T(8,128)(2,1)S(1)} %get-tuple-element.143), channel_id=1, source_target_pairs={{16,0},{32,16},{48,32},{0,48},{80,64},{96,80},{112,96},{64,112},{1... | collective-permute-start | bytes 786440 | tf_op jit(solution)/shard_map/ppermute | solution.py:549

commit v2 on v1

--- a/solution.py
+++ b/solution.py
@@ -73,26 +73,21 @@
     tgt_ref[...] = jnp.where(where_last >= width - 4, tail, where.astype(I32))
 
 
-def prep_kernel(meta, rows_hbm, cols_hbm, vals, *refs):
-    list_a, tgt_a, list_b, tgt_b, held, rows, cols, sems, id_sems = refs
+def list_kernel(forward, meta, rows, cols, *refs):
     live, y_hi, z, y_lo, x, core = [meta[i] for i in range(6)]
-    ids = [
-        pltpu.make_async_copy(rows_hbm, rows, id_sems.at[0]),
-        pltpu.make_async_copy(cols_hbm, cols, id_sems.at[1]),
-    ]
-    chunks = [
-        pltpu.make_async_copy(
-            vals.at[pl.ds(LOAD * i, LOAD)], held.at[pl.ds(LOAD * i, LOAD)], sems.at[i]
-        )
-        for i in range(SLOTS // LOAD)
-    ]
-    for copy in ids:
-        copy.start()
+    chunks = []
+    if forward:
+        vals, list_ref, tgt_ref, held, sems = refs
+        chunks = [
+            pltpu.make_async_copy(
+                vals.at[pl.ds(LOAD * i, LOAD)], held.at[pl.ds(LOAD * i, LOAD)], sems.at[i]
+            )
+            for i in range(SLOTS // LOAD)
+        ]
+    else:
+        list_ref, tgt_ref = refs
     for i, chunk in enumerate(chunks):
         pl.when(LOAD * i < live)(chunk.start)
-    for copy in ids:
-        copy.wait()
-
     row = rows[...]
     col = cols[...]
     used = lax.broadcasted_iota(I32, (1, SLOTS), 1) < live
@@ -114,40 +109,31 @@
     col_early = (dyh == 0) & (dz != 2)
     place = jnp.where(col_early, (dz + 1) >> 1, jnp.where(dyh == 1, 1 + dz, 0))
     col_source = place * 4 + (col & 3)
-    row_target = jnp.where(col_early, row_target, 64 + row_target)
-    col_target = jnp.where(row_early, col_target, 32 + col_target)
-    sort_slots(2, (0, 64, 96, 104, 128), used, row_target, col_source, 20, list_a, tgt_a)
-    sort_slots(2, (0, 32, 48, 56, 64), used, col_target, row_source, 32, list_b, tgt_b)
-
+    if forward:
+        target = jnp.where(col_early, row_target, 64 + row_target)
+        sort_slots(2, (0, 64, 96, 104, 128), used, target, col_source, 20, list_ref, tgt_ref)
+    else:
+        target = jnp.where(row_early, col_target, 32 + col_target)
+        sort_slots(2, (0, 32, 48, 56, 64), used, target, row_source, 32, list_ref, tgt_ref)
     for i, chunk in enumerate(chunks):
         pl.when(LOAD * i < live)(chunk.wait)
 
 
-def prep(meta, rows, cols, vals):
-    tgts = pltpu.VMEM((1, 384), I32)
-    return pl.pallas_call(
-        prep_kernel,
-        out_shape=(
-            pltpu.VMEM((1, 640), I32),
-            tgts,
-            pltpu.VMEM((1, 640), I32),
-            tgts,
-            pltpu.VMEM((SLOTS, BLK, BLK), BF16),
-        ),
-        in_specs=[SMEM_SPEC] + [ANY_SPEC] * 3,
-        out_specs=[VMEM_SPEC] * 5,
-        scratch_shapes=[
-            pltpu.VMEM((1, SLOTS), I32),
-            pltpu.VMEM((1, SLOTS), I32),
-            pltpu.SemaphoreType.DMA((SLOTS // LOAD,)),
-            pltpu.SemaphoreType.DMA((2,)),
-        ],
-        compiler_params=pltpu.CompilerParams(vmem_limit_bytes=44 * MIB),
-        cost_estimate=pl.CostEstimate(
-            flops=2**20, bytes_accessed=SLOTS * BLK * BLK * 2, transcendentals=0
-        ),
-        name="slot_lists",
-    )(meta, rows, cols, vals)
+def slot_list(meta, rows, cols, vals=None):
+    forward = vals is not None
+    out = [pltpu.VMEM((1, 640), I32), pltpu.VMEM((1, 384), I32)]
+    if forward:
+        out.append(pltpu.VMEM((SLOTS, BLK, BLK), BF16))
+    return pl.pallas_call(
+        functools.partial(list_kernel, forward),
+        out_shape=out,
+        in_specs=[SMEM_SPEC, VMEM_SPEC, VMEM_SPEC] + [ANY_SPEC] * forward,
+        out_specs=[VMEM_SPEC] * len(out),
+        scratch_shapes=[pltpu.SemaphoreType.DMA((SLOTS // LOAD,))] * forward,
+        compiler_params=pltpu.CompilerParams(vmem_limit_bytes=(44 if forward else 8) * MIB),
+        cost_estimate=pl.CostEstimate(flops=2**20, bytes_accessed=8 * MIB, transcendentals=0),
+        name="slot_list_forward" if forward else "slot_list_backward",
+    )(meta, rows, cols, *([vals] if forward else []))
 
 
 def start_pieces(places, pieces, field, sems):
@@ -405,7 +391,7 @@
 
 def dense_kernel(norm, *refs):
     parts = refs[:4]
-    weight, bias, upstream, activation, mid, terms = refs[4:]
+    meta, weight, bias, upstream, activation, mid, keep, send, scratch = refs[4:]
     w = weight[...]
     w_term = jnp.zeros((F, F), F32)
     b_term = jnp.zeros((1, F), F32)
@@ -428,26 +414,32 @@
             aggregated, grad_pre, (((0,), (0,)), ((), ())), preferred_element_type=F32
         )
         b_term += jnp.sum(grad_pre.astype(F32), axis=0, keepdims=True)
-    terms[pl.ds(0, F), :] = w_term * norm
-    terms[pl.ds(F, 8), :] = jnp.broadcast_to(b_term * norm, (8, F))
-
-
-def dense(parts, weight, bias, upstream, norm):
+    scratch[...] = w_term * norm
+    core = meta[5]
+    b_rows = jnp.broadcast_to(b_term * norm, (8, F))
+    for half, which in ((keep, core), (send, 1 - core)):
+        half[pl.ds(0, BLK), :] = scratch[pl.ds(pl.multiple_of(which * BLK, BLK), BLK), :]
+        half[pl.ds(BLK, 8), :] = b_rows
+
+
+def dense(parts, meta, weight, bias, upstream, norm):
     return pl.pallas_call(
         functools.partial(dense_kernel, norm),
         out_shape=(
             jax.ShapeDtypeStruct((4 * BLK, F), BF16),
             jax.ShapeDtypeStruct((4, F, BLK), BF16),
-            jax.ShapeDtypeStruct((F + 8, F), F32),
+            jax.ShapeDtypeStruct((BLK + 8, F), F32),
+            jax.ShapeDtypeStruct((BLK + 8, F), F32),
         ),
-        in_specs=[VMEM_SPEC] * 7,
-        out_specs=[VMEM_SPEC] * 3,
+        in_specs=[VMEM_SPEC] * 4 + [SMEM_SPEC] + [VMEM_SPEC] * 3,
+        out_specs=[VMEM_SPEC] * 4,
+        scratch_shapes=[pltpu.VMEM((F, F), F32)],
         compiler_params=pltpu.CompilerParams(vmem_limit_bytes=12 * MIB),
         cost_estimate=pl.CostEstimate(
             flops=6 * 512 * F * F, bytes_accessed=4 * 2**20, transcendentals=512 * F
         ),
         name="dense_layer",
-    )(*parts, weight, bias.reshape(1, F), upstream)
+    )(*parts, meta, weight, bias.reshape(1, F), upstream)
 
 
 def across_kernel(own, across, out):
@@ -462,21 +454,24 @@
         in_specs=[VMEM_SPEC] * 2,
         out_specs=VMEM_SPEC,
         compiler_params=pltpu.CompilerParams(vmem_limit_bytes=8 * MIB),
-        cost_estimate=pl.CostEstimate(flops=10**10, bytes_accessed=MIB, transcendentals=0),
+        cost_estimate=pl.CostEstimate(flops=4 * 10**10, bytes_accessed=MIB, transcendentals=0),
         name="add_across",
     )(own, across)
 
 
-def finish_kernel(here, up, down, mine, theirs, grad, w_grad, b_grad):
+def finish_kernel(here, up, down, meta, *refs):
+    mine, theirs, mate, mate_theirs, grad, w_grad, b_grad = refs
     for i in range(4):
         total = here[i] + (up[i].astype(F32) + down[i].astype(F32))
         grad[pl.ds(BLK * i, BLK), :] = total.T.astype(BF16)
-    total = mine[...].astype(F32) + theirs[...].astype(F32)
-    w_grad[...] = total[:F]
-    b_grad[...] = total[F : F + 1]
-
-
-def finish(here, up, down, mine, theirs):
+    core = meta[5]
+    for one, two, which in ((mine, theirs, core), (mate, mate_theirs, 1 - core)):
+        total = one[...].astype(F32) + two[...].astype(F32)
+        w_grad[pl.ds(pl.multiple_of(which * BLK, BLK), BLK), :] = total[:BLK]
+    b_grad[...] = total[BLK : BLK + 1]
+
+
+def finish(here, up, down, meta, *terms):
     return pl.pallas_call(
         finish_kernel,
         out_shape=(
@@ -484,11 +479,11 @@
             jax.ShapeDtypeStruct((F, F), F32),
             jax.ShapeDtypeStruct((1, F), F32),
         ),
-        in_specs=[VMEM_SPEC] * 5,
+        in_specs=[VMEM_SPEC] * 3 + [SMEM_SPEC] + [VMEM_SPEC] * 4,
         out_specs=[VMEM_SPEC] * 3,
         compiler_params=pltpu.CompilerParams(vmem_limit_bytes=8 * MIB),
         name="finish_grads",
-    )(here, up, down, mine, theirs)
+    )(here, up, down, meta, *terms)
 
 
 def halves_kernel(*refs):
@@ -574,12 +569,13 @@
     meta = jnp.stack(
         [live_count[0, 0], row >> 2, row & 3, col >> 3, (col >> 1) & 3, col & 1, row, col]
     ).astype(I32)
-    list_a, tgt_a, list_b, tgt_b, held = prep(meta, block_rows, block_cols, vals)
-
     shard = features.reshape(4, BLK, F)
+    list_a, tgt_a, held = slot_list(meta, block_rows, block_cols, vals)
+    list_b, tgt_b = slot_list(meta, block_rows, block_cols)
+
     other = from_row(shard, 1, 0)
     up, down = from_row(shard, 0, 1), from_row(shard, 0, 3)
-    up, down, other, list_a = tie(up, down, other, list_a)
+    other, up, down, list_a = tie(other, up, down, list_a)
     up2, down2 = from_row(other, 0, 1), from_row(other, 0, 3)
     late = [from_row(up[:2], 0, 1), from_row(down[2:], 0, 3), other]
     early = early_product(
@@ -608,13 +604,13 @@
     up1, down1, up0, down0, own = relay(keep_near, got_near, low, high)
     up1, down1 = from_col(up1, 0, 0, 3), from_col(down1, 0, 0, 1)
     across = (own[1] + up1.astype(F32) + down1.astype(F32)).astype(BF16)
-    up0, down0, across = tie(up0, down0, across)
+    up0, down0, across, list_b = tie(up0, down0, across, list_b)
     across = from_col(across, 0, 1, 0)
     up0, down0 = from_col(up0, 0, 0, 3), from_col(down0, 0, 0, 1)
 
     nodes = 4 * BLK * lax.axis_size("row") * lax.axis_size("col")
-    activation, mid, terms = dense(
-        [own, up0, down0, across], weight, bias_term, upstream, float(nodes) ** -0.5
+    activation, mid, keep, send = dense(
+        [own, up0, down0, across], meta, weight, bias_term, upstream, float(nodes) ** -0.5
     )
 
     def pair(value, axis, kind, bit):
@@ -630,7 +626,7 @@
 
     up, down = from_col(mid, 0, 0, 1), from_col(mid, 0, 0, 3)
     other = from_col(mid, 0, 1, 0)
-    terms1 = add(*pair(terms, "col", F32, 1))
+    terms1 = keep + core(send)
     other, terms1 = tie(other, terms1)
     mine, theirs = pair(terms1, "row", F32, 1)
     up2 = from_col(join(other, up[:2]), 0, 0, 1)
@@ -651,6 +647,7 @@
     up2, down2, terms2 = tie(up2, down2, add(mine, theirs))
     mine, theirs = pair(terms2, "col", F32, 8)
     low, high = from_col(up2[:2], 0, 0, 1), from_col(down2[2:4], 0, 0, 3)
+    low, high, theirs = tie(low, high, theirs)
     late = [up2, down2, low, high, core(join(up2, down2)), core(join(low, high))]
     list_b1, terms3 = tie(list_b, add(mine, theirs))
     mine, theirs = pair(terms3, "row", BF16, 2)
@@ -672,10 +669,13 @@
     across = (own1 + up1[:4].astype(F32) + down1[:4].astype(F32)).astype(BF16)
     across = from_row(across, 1, 0)
     up0, down0 = add_halves(up0, down0, up1[4:], down1[4:])
+    up0, down0, theirs = tie(up0, down0, theirs)
     up0, down0 = from_row(up0, 0, 3), from_row(down0, 0, 1)
-    mine, theirs = pair(add(mine, theirs), "col", BF16, 4)
+    mine = add(mine, theirs).astype(BF16)
+    mine, mate = tie(mine, core(mine))
+    theirs, mate_theirs = pair(mine, "col", BF16, 4)[1], pair(mine, "col", BF16, 5)[1]
     here = add_across(own0, across)
-    feature_grad, weight_grad, bias_grad = finish(here, up0, down0, mine, theirs)
+    feature_grad, weight_grad, bias_grad = finish(here, up0, down0, meta, mine, theirs, mate, mate_theirs)
     return (activation, feature_grad, weight_grad, bias_grad.reshape(F))
 
 

time: 146 us -> 147 us (level)
  starting transfers between devices: 60.1 us -> 49.5 us
  waiting for transfers between devices: 55.1 us -> 61.1 us
  Pallas kernels: 27 us -> 32.8 us
    ppermute x20 -> x22, starting transfers between devices: 25.8 us -> 17.5 us  [from_col(): lax.ppermute(value, 'col', [(col_peer(c, dcore, dy, dx), c) for c in rang...]
    ppermute x7, waiting for transfers between devices: 17.6 us -> 9.83 us  [pair(): return (value, lax.ppermute(value, axis, peers))]
    ppermute x16, waiting for transfers between devices: 8.25 us -> 15.6 us  [from_row(): return lax.ppermute(value, 'row', perm)]
    ppermute x20 -> x22, waiting for transfers between devices: 29.2 us -> 35.7 us  [from_col(): lax.ppermute(value, 'col', [(col_peer(c, dcore, dy, dx), c) for c in rang...]
    ppermute x16, starting transfers between devices: 28.7 us -> 26 us  [from_row(): return lax.ppermute(value, 'row', perm)]
    pallas_call x2, Pallas kernels: 6.51 us -> 8.93 us  [early_product(): pl.pallas_call(functools.partial(early_kernel, places, forward), out_shap...]
    pallas_call x1 -> x2, Pallas kernels: 4.43 us -> 5.39 us  [slot_list(): pl.pallas_call(functools.partial(list_kernel, forward), out_shape=out, in...]
  transfers between devices with their start and end apart: 43 -> 45, of which waited for: 22 -> 26; matrix products, arithmetic and copies ran while one was open for 1% -> 1% of each run, Pallas kernels for 14% -> 17%
where the time goes in v2:
time: 147 us
  waiting for transfers between devices  61.1 us (42%)
  starting transfers between devices  49.5 us (34%)
  Pallas kernels  32.8 us (22%)
  between operations  1.72 us (1%)
    ppermute x22, waiting for transfers between devices, from_col(): lax.ppermute(value, 'col', [(col_peer(c, dcore, dy, dx), c) for c in rang...  35.7 us
    ppermute x16, starting transfers between devices, from_row(): return lax.ppermute(value, 'row', perm)  26 us
    ppermute x22, starting transfers between devices, from_col(): lax.ppermute(value, 'col', [(col_peer(c, dcore, dy, dx), c) for c in rang...  17.5 us
    ppermute x16, waiting for transfers between devices, from_row(): return lax.ppermute(value, 'row', perm)  15.6 us
    pallas_call x6, Pallas kernels, product_call(): pl.pallas_call(kernel, out_shape=out_shape, in_specs=[SMEM_SPEC] * 2 + [V...  14.4 us
    ppermute x7, waiting for transfers between devices, pair(): return (value, lax.ppermute(value, axis, peers))  9.83 us
    pallas_call x2, Pallas kernels, early_product(): pl.pallas_call(functools.partial(early_kernel, places, forward), out_shap...  8.93 us
    ppermute x7, starting transfers between devices, pair(): return (value, lax.ppermute(value, axis, peers))  5.97 us
  transfers between devices with their start and end apart: 45, of which 26 were waited for; matrix products, arithmetic and copies ran while one was open for 1% of the time, Pallas kernels for 17%

profile of v2, /device:TPU:0, one launch (start us, length us, event | category | flops | bytes accessed | tf_op | source)
XLA Modules:
  0.0 146.7 jit_solution(1122357388389635598)
XLA Ops:
  0.6 3.4 %collective-permute-start = (bf16[4,128,256]{2,1,0:T(8,128)(2,1)}, bf16[4,128,256]{2,1,0:T(8,128)(2,1)S(1)}, u32[]{:S(2)}, u32[]{:S(2)}) collective-permute-start(bf16[4,128,256]{2,1,0:T(8,128)(2,1)} %bitcast.21), channel_id=1, source_target_pairs={{64,0},{80,16},{96,32},{112,48},{0,64},{16,80},{32,96},{48,112},{6... | collective-permute-start | bytes 786440 | tf_op jit(solution)/shard_map/ppermute | solution.py:544
  4.0 4.0 %collective-permute-start.1 = (bf16[4,128,256]{2,1,0:T(8,128)(2,1)}, bf16[4,128,256]{2,1,0:T(8,128)(2,1)S(1)}, u32[]{:S(2)}, u32[]{:S(2)}) collective-permute-start(bf16[4,128,256]{2,1,0:T(8,128)(2,1)} %bitcast.22), channel_id=1, source_target_pairs={{16,0},{32,16},{48,32},{0,48},{80,64},{96,80},{112,96},{64,112},{1... | collective-permute-start | bytes 786440 | tf_op jit(solution)/shard_map/ppermute | solution.py:544
  8.7 0.7 stack.31.meta.refs_4_
  9.4 4.0 %slot_list_forward.1 = (s32[1,640]{1,0:T(1,128)S(1)}, s32[1,384]{1,0:T(1,128)S(1)}, bf16[384,128,128]{2,1,0:T(8,128)(2,1)S(1)}) custom-call(s32[8]{0:T(128)} %stack.31.meta.refs_4_, s32[1,384]{1,0:T(1,128)} %rows.3, s32[1,384]{1,0:T(1,128)} %cols.3, bf16[384,128,128]{2,1,0:T(8,128)(2,1)} %bitcast.26), custom_call_target="tpu_custom_call" | custom-call | flops 1048576 | bytes 8388608 | tf_op jit(solution)/shard_map/slot_list_forward/pallas_call | solution.py:127
  13.6 3.3 %collective-permute-done.2.refs_2_ = bf16[4,128,256]{2,1,0:T(8,128)(2,1)S(1)} collective-permute-done((bf16[4,128,256]{2,1,0:T(8,128)(2,1)}, bf16[4,128,256]{2,1,0:T(8,128)(2,1)S(1)}, u32[]{:S(2)}, u32[]{:S(2)}) %collective-permute-start.2) | collective-permute-done | bytes 262176 | tf_op jit(solution)/shard_map/ppermute | solution.py:544
  16.9 1.0 collective-permute-start.3
  17.9 1.1 collective-permute-start.4
  19.0 2.2 %collective-permute-start.5 = (bf16[2,128,256]{2,1,0:T(8,128)(2,1)S(1)}, bf16[2,128,256]{2,1,0:T(8,128)(2,1)S(1)}, u32[]{:S(2)}, u32[]{:S(2)}) collective-permute-start(bf16[2,128,256]{2,1,0:T(8,128)(2,1)S(1)} %slice.45), channel_id=1, source_target_pairs={{16,0},{32,16},{48,32},{0,48},{80,64},{96,80},{112,96},{64,112},{1... | collective-permute-start | bytes 393224 | tf_op jit(solution)/shard_map/ppermute | solution.py:544
  21.3 4.1 %forward_early.1.early = f32[64,128,256]{2,1,0:T(8,128)S(1)} custom-call(s32[1,640]{1,0:T(1,128)S(1)} %get-tuple-element.98.list_ref, s32[1,384]{1,0:T(1,128)S(1)} %get-tuple-element.88.tgt_ref, bf16[384,128,128]{2,1,0:T(8,128)(2,1)S(1)} %get-tuple-element.89.held, bf16[4,128,256]{2,1,0:T(8,128)(2,1)S(1)} %bitcast.24, ...), custom_call_target="tpu_custom_call" | custom-call | flops 1610612736 | bytes 12582912 | tf_op jit(solution)/shard_map/forward_early/pallas_call | solution.py:228
  25.4 1.2 collective-permute-done.4.refs_6_
  26.6 3.1 %collective-permute-start.7 = (bf16[2,128,256]{2,1,0:T(8,128)(2,1)S(1)}, bf16[2,128,256]{2,1,0:T(8,128)(2,1)S(1)}, u32[]{:S(2)}, u32[]{:S(2)}) collective-permute-start(bf16[2,128,256]{2,1,0:T(8,128)(2,1)S(1)} %slice.47), channel_id=1, source_target_pairs={{16,0},{32,16},{48,32},{0,48},{80,64},{96,80},{112,96},{64,112},{1... | collective-permute-start | bytes 393224 | tf_op jit(solution)/shard_map/ppermute | solution.py:544
  29.8 2.4 %collective-permute-done.7.refs_4_ = bf16[2,128,256]{2,1,0:T(8,128)(2,1)S(1)} collective-permute-done((bf16[2,128,256]{2,1,0:T(8,128)(2,1)S(1)}, bf16[2,128,256]{2,1,0:T(8,128)(2,1)S(1)}, u32[]{:S(2)}, u32[]{:S(2)}) %collective-permute-start.7) | collective-permute-done | bytes 131104 | tf_op jit(solution)/shard_map/ppermute | solution.py:544
  32.2 3.7 %collective-permute-done.8.refs_5_ = bf16[2,128,256]{2,1,0:T(8,128)(2,1)S(1)} collective-permute-done((bf16[2,128,256]{2,1,0:T(8,128)(2,1)S(1)}, bf16[2,128,256]{2,1,0:T(8,128)(2,1)S(1)}, u32[]{:S(2)}, u32[]{:S(2)}) %collective-permute-start.8) | collective-permute-done | bytes 131104 | tf_op jit(solution)/shard_map/ppermute | solution.py:544
  36.0 3.7 %forward_other_core.1 = (bf16[2,4,128,256]{3,2,1,0:T(8,128)(2,1)S(1)}, bf16[2,3,4,128,256]{4,3,2,1,0:T(8,128)(2,1)S(1)}, bf16[21,128,256]{2,1,0:T(8,128)(2,1)S(1)}) custom-call(s32[1,640]{1,0:T(1,128)S(1)} %get-tuple-element.98.list_ref, s32[1,384]{1,0:T(1,128)S(1)} %get-tuple-element.88.tgt_ref, bf16[384,128,128]{2,1,0:T(8,128)(2,1)S(1)} %get-tuple-element.89.held, ...), custom_call_target="tpu_custom_call" | custom-call | flops 1610612736 | bytes 12582912 | tf_op jit(solution)/shard_map/forward_other_core/pallas_call | solution.py:257
  39.8 0.5 collective-permute-start.9
  40.3 1.3 forward_own_far.1
  41.6 2.3 %collective-permute-done.9 = bf16[2,4,128,256]{3,2,1,0:T(8,128)(2,1)S(1)} collective-permute-done((bf16[2,4,128,256]{3,2,1,0:T(8,128)(2,1)S(1)}, bf16[2,4,128,256]{3,2,1,0:T(8,128)(2,1)S(1)}, u32[]{:S(2)}, u32[]{:S(2)}) %collective-permute-start.9) | collective-permute-done | bytes 524320 | tf_op jit(solution)/shard_map/ppermute | solution.py:552
  44.2 3.2 %collective-permute-start.12 = (bf16[2,2,128,256]{3,2,1,0:T(8,128)(2,1)S(1)}, bf16[2,2,128,256]{3,2,1,0:T(8,128)(2,1)S(1)}, u32[]{:S(2)}, u32[]{:S(2)}) collective-permute-start(bf16[2,2,128,256]{3,2,1,0:T(8,128)(2,1)S(1)} %get-tuple-element.101), channel_id=1, source_target_pairs={{2,0},{3,1},{4,2},{5,3},{6,4},{7,5},{0,6},{1,7},{10,8},{11,9},{12,... | collective-permute-start | bytes 786440 | tf_op jit(solution)/shard_map/ppermute | solution.py:552
  47.4 2.1 %forward_own_near.1.keep = f32[24,128,256]{2,1,0:T(8,128)S(1)} custom-call(s32[1,640]{1,0:T(1,128)S(1)} %get-tuple-element.98.list_ref, s32[1,384]{1,0:T(1,128)S(1)} %get-tuple-element.88.tgt_ref, bf16[384,128,128]{2,1,0:T(8,128)(2,1)S(1)} %get-tuple-element.89.held, f32[64,128,256]{2,1,0:T(8,128)S(1)} %forward_early.1.early, ...), custom_call_target="tpu_custom_call" | custom-call | flops 1610612736 | bytes 12582912 | tf_op jit(solution)/shard_map/forward_own_near/pallas_call | solution.py:257
  49.6 4.1 %collective-permute-done.11.low = bf16[2,2,128,256]{3,2,1,0:T(8,128)(2,1)S(1)} collective-permute-done((bf16[2,2,128,256]{3,2,1,0:T(8,128)(2,1)S(1)}, bf16[2,2,128,256]{3,2,1,0:T(8,128)(2,1)S(1)}, u32[]{:S(2)}, u32[]{:S(2)}) %collective-permute-start.11) | collective-permute-done | bytes 262176 | tf_op jit(solution)/shard_map/ppermute | solution.py:552
  53.8 0.4 relay_sums.1
  54.3 3.2 %collective-permute-start.14 = (bf16[4,128,256]{2,1,0:T(8,128)(2,1)S(1)}, bf16[4,128,256]{2,1,0:T(8,128)(2,1)S(1)}, u32[]{:S(2)}, u32[]{:S(2)}) collective-permute-start(bf16[4,128,256]{2,1,0:T(8,128)(2,1)S(1)} %get-tuple-element.106), channel_id=1, source_target_pairs={{2,0},{3,1},{4,2},{5,3},{6,4},{7,5},{0,6},{1,7},{10,8},{11,9},{12,... | collective-permute-start | bytes 786440 | tf_op jit(solution)/shard_map/ppermute | solution.py:552
  57.5 1.4 slot_list_backward.1
  58.9 4.1 %collective-permute-done.13 = bf16[4,128,256]{2,1,0:T(8,128)(2,1)S(1)} collective-permute-done((bf16[4,128,256]{2,1,0:T(8,128)(2,1)S(1)}, bf16[4,128,256]{2,1,0:T(8,128)(2,1)S(1)}, u32[]{:S(2)}, u32[]{:S(2)}) %collective-permute-start.13) | collective-permute-done | bytes 262176 | tf_op jit(solution)/shard_map/ppermute | solution.py:552
  63.1 0.9 collective-permute-start.15
  64.0 2.4 %collective-permute-start.16 = (bf16[4,128,256]{2,1,0:T(8,128)(2,1)S(1)}, bf16[4,128,256]{2,1,0:T(8,128)(2,1)S(1)}, u32[]{:S(2)}, u32[]{:S(2)}) collective-permute-start(bf16[4,128,256]{2,1,0:T(8,128)(2,1)S(1)} %get-tuple-element.109), channel_id=1, source_target_pairs={{2,0},{3,1},{4,2},{5,3},{6,4},{7,5},{0,6},{1,7},{10,8},{11,9},{12,... | collective-permute-start | bytes 786440 | tf_op jit(solution)/shard_map/ppermute | solution.py:552
  66.4 4.6 %collective-permute-done.15.refs_1_ = bf16[4,128,256]{2,1,0:T(8,128)(2,1)S(1)} collective-permute-done((bf16[4,128,256]{2,1,0:T(8,128)(2,1)S(1)}, bf16[4,128,256]{2,1,0:T(8,128)(2,1)S(1)}, u32[]{:S(2)}, u32[]{:S(2)}) %collective-permute-start.15) | collective-permute-done | bytes 262176 | tf_op jit(solution)/shard_map/ppermute | solution.py:552
  71.0 1.8 %collective-permute-done.17.refs_3_ = bf16[4,128,256]{2,1,0:T(8,128)(2,1)S(1)} collective-permute-done((bf16[4,128,256]{2,1,0:T(8,128)(2,1)S(1)}, bf16[4,128,256]{2,1,0:T(8,128)(2,1)S(1)}, u32[]{:S(2)}, u32[]{:S(2)}) %collective-permute-start.17) | collective-permute-done | bytes 262176 | tf_op jit(solution)/shard_map/ppermute | solution.py:552
  72.8 2.0 %dense_layer.1 = (bf16[512,256]{1,0:T(8,128)(2,1)}, bf16[4,256,128]{2,1,0:T(8,128)(2,1)S(1)}, f32[136,256]{1,0:T(8,128)S(1)}, f32[136,256]{1,0:T(8,128)S(1)}) custom-call(f32[2,4,128,256]{3,2,1,0:T(8,128)S(1)} %get-tuple-element.102.refs_0_, bf16[4,128,256]{2,1,0:T(8,128)(2,1)S(1)} %collective-permute-done.15.refs_1_, ...), custom_call_target="tpu_custom_call" | custom-call | flops 201326592 | bytes 4194304 | tf_op jit(solution)/shard_map/dense_layer/pallas_call | solution.py:426
  74.8 1.7 %collective-permute-start.20 = (bf16[4,256,128]{2,1,0:T(8,128)(2,1)S(1)}, bf16[4,256,128]{2,1,0:T(8,128)(2,1)S(1)}, u32[]{:S(2)}, u32[]{:S(2)}) collective-permute-start(bf16[4,256,128]{2,1,0:T(8,128)(2,1)S(1)} %get-tuple-element.113.refs_0_), channel_id=1, source_target_pairs={{2,0},{3,1},{4,2},{5,3},{6,4},{7,5},{0,6},{1,7},{10,8},{11,9},{12,... | collective-permute-start | bytes 786440 | tf_op jit(solution)/shard_map/ppermute | solution.py:552
  76.6 0.3 collective-permute-start.22
  76.8 1.4 collective-permute-done.19
  78.2 3.0 %collective-permute-done.18.refs_3_ = bf16[4,256,128]{2,1,0:T(8,128)(2,1)S(1)} collective-permute-done((bf16[4,256,128]{2,1,0:T(8,128)(2,1)S(1)}, bf16[4,256,128]{2,1,0:T(8,128)(2,1)S(1)}, u32[]{:S(2)}, u32[]{:S(2)}) %collective-permute-start.18) | collective-permute-done | bytes 262176 | tf_op jit(solution)/shard_map/ppermute | solution.py:552
  81.2 3.0 %collective-permute-done.22.refs_2_ = bf16[4,256,128]{2,1,0:T(8,128)(2,1)S(1)} collective-permute-done((bf16[4,256,128]{2,1,0:T(8,128)(2,1)S(1)}, bf16[4,256,128]{2,1,0:T(8,128)(2,1)S(1)}, u32[]{:S(2)}, u32[]{:S(2)}) %collective-permute-start.22) | collective-permute-done | bytes 262176 | tf_op jit(solution)/shard_map/ppermute | solution.py:552
  84.3 0.5 collective-permute-start.25
  85.0 2.0 %collective-permute-start.23 = (bf16[6,256,128]{2,1,0:T(8,128)(2,1)S(1)}, bf16[6,256,128]{2,1,0:T(8,128)(2,1)S(1)}, u32[]{:S(2)}, u32[]{:S(2)}) collective-permute-start(bf16[6,256,128]{2,1,0:T(8,128)(2,1)S(1)} %get-tuple-element.170), channel_id=1, source_target_pairs={{6,0},{7,1},{0,2},{1,3},{2,4},{3,5},{4,6},{5,7},{14,8},{15,9},{8,1... | collective-permute-start | bytes 1179656 | tf_op jit(solution)/shard_map/ppermute | solution.py:552
  87.0 4.9 %backward_early.1.early = f32[32,256,128]{2,1,0:T(8,128)S(1)} custom-call(s32[1,640]{1,0:T(1,128)S(1)} %get-tuple-element.150.list_ref, s32[1,384]{1,0:T(1,128)S(1)} %get-tuple-element.118.tgt_ref, bf16[384,128,128]{2,1,0:T(8,128)(2,1)S(1)} %get-tuple-element.89.held, bf16[4,256,128]{2,1,0:T(8,128)(2,1)S(1)} %get-tuple-element.113.refs_0_, ...), custom_call_target="tpu_custom_call" | custom-call | flops 1610612736 | bytes 12582912 | tf_op jit(solution)/shard_map/backward_early/pallas_call | solution.py:228
  92.1 4.0 %collective-permute-done.21.refs_0_ = bf16[6,256,128]{2,1,0:T(8,128)(2,1)S(1)} collective-permute-done((bf16[6,256,128]{2,1,0:T(8,128)(2,1)S(1)}, bf16[6,256,128]{2,1,0:T(8,128)(2,1)S(1)}, u32[]{:S(2)}, u32[]{:S(2)}) %collective-permute-start.21) | collective-permute-done | bytes 393248 | tf_op jit(solution)/shard_map/ppermute | solution.py:552
  96.1 1.3 collective-permute-done.23.refs_1_
  97.6 2.1 %collective-permute-start.29 = (f32[136,256]{1,0:T(8,128)S(1)}, f32[136,256]{1,0:T(8,128)S(1)}, u32[]{:S(2)}, u32[]{:S(2)}) collective-permute-start(f32[136,256]{1,0:T(8,128)S(1)} %add.37), channel_id=1, source_target_pairs={{8,0},{9,1},{10,2},{11,3},{12,4},{13,5},{14,6},{15,7},{0,8},{1,9},... | collective-permute-start | bytes 417800 | tf_op jit(solution)/shard_map/ppermute | solution.py:619
  99.7 0.3 collective-permute-start.27
  100.0 1.8 %collective-permute-start.28 = (bf16[2,256,128]{2,1,0:T(8,128)(2,1)S(1)}, bf16[2,256,128]{2,1,0:T(8,128)(2,1)S(1)}, u32[]{:S(2)}, u32[]{:S(2)}) collective-permute-start(bf16[2,256,128]{2,1,0:T(8,128)(2,1)S(1)} %slice.55), channel_id=1, source_target_pairs={{6,0},{7,1},{0,2},{1,3},{2,4},{3,5},{4,6},{5,7},{14,8},{15,9},{8,1... | collective-permute-start | bytes 393224 | tf_op jit(solution)/shard_map/ppermute | solution.py:552
  101.8 3.5 %collective-permute-done.27.refs_2_ = bf16[2,256,128]{2,1,0:T(8,128)(2,1)S(1)} collective-permute-done((bf16[2,256,128]{2,1,0:T(8,128)(2,1)S(1)}, bf16[2,256,128]{2,1,0:T(8,128)(2,1)S(1)}, u32[]{:S(2)}, u32[]{:S(2)}) %collective-permute-start.27) | collective-permute-done | bytes 131104 | tf_op jit(solution)/shard_map/ppermute | solution.py:552
  105.3 1.3 collective-permute-done.28.refs_3_
  106.9 1.4 collective-permute-done.31.refs_5_
  108.3 4.0 %backward_across.1 = (f32[4,256,128]{2,1,0:T(8,128)S(1)}, bf16[4,256,128]{2,1,0:T(8,128)(2,1)S(1)}, bf16[4,256,128]{2,1,0:T(8,128)(2,1)S(1)}, bf16[2,256,128]{2,...) custom-call(s32[1,640]{1,0:T(1,128)S(1)} %get-tuple-element.150.list_ref, ...), custom_call_target="tpu_custom_call" | custom-call | flops 1610612736 | bytes 12582912 | tf_op jit(solution)/shard_map/backward_across/pallas_call | solution.py:257
  112.4 3.2 %collective-permute-start.35 = (bf16[2,256,128]{2,1,0:T(8,128)(2,1)S(1)}, bf16[2,256,128]{2,1,0:T(8,128)(2,1)S(1)}, u32[]{:S(2)}, u32[]{:S(2)}) collective-permute-start(bf16[2,256,128]{2,1,0:T(8,128)(2,1)S(1)} %get-tuple-element.142), channel_id=1, source_target_pairs={{16,0},{32,16},{48,32},{0,48},{80,64},{96,80},{112,96},{64,112},{1... | collective-permute-start | bytes 393224 | tf_op jit(solution)/shard_map/ppermute | solution.py:544
  115.6 0.7 collective-permute-start.33
  116.3 1.6 %backward_far_own.1 = (bf16[2,256,128]{2,1,0:T(8,128)(2,1)S(1)}, bf16[2,256,128]{2,1,0:T(8,128)(2,1)S(1)}, f32[4,256,128]{2,1,0:T(8,128)S(1)}) custom-call(s32[1,640]{1,0:T(1,128)S(1)} %get-tuple-element.150.list_ref, s32[1,384]{1,0:T(1,128)S(1)} %get-tuple-element.118.tgt_ref, bf16[384,128,128]{2,1,0:T(8,128)(2,1)S(1)} %get-tuple-element.89.held, ...), custom_call_target="tpu_custom_call" | custom-call | flops 1610612736 | bytes 12582912 | tf_op jit(solution)/shard_map/backward_far_own/pallas_call | solution.py:257
  118.0 1.1 collective-permute-done.34.refs_2_
  119.2 2.3 %collective-permute-done.33 = bf16[136,256]{1,0:T(8,128)(2,1)S(1)} collective-permute-done((bf16[136,256]{1,0:T(8,128)(2,1)S(1)}, bf16[136,256]{1,0:T(8,128)(2,1)S(1)}, u32[]{:S(2)}, u32[]{:S(2)}) %collective-permute-start.33) | collective-permute-done | bytes 69664 | tf_op jit(solution)/shard_map/ppermute | solution.py:619
  121.5 3.2 %collective-permute-start.37 = (bf16[6,256,128]{2,1,0:T(8,128)(2,1)S(1)}, bf16[6,256,128]{2,1,0:T(8,128)(2,1)S(1)}, u32[]{:S(2)}, u32[]{:S(2)}) collective-permute-start(bf16[6,256,128]{2,1,0:T(8,128)(2,1)S(1)} %get-tuple-element.148), channel_id=1, source_target_pairs={{16,0},{32,16},{48,32},{0,48},{80,64},{96,80},{112,96},{64,112},{1... | collective-permute-start | bytes 1179656 | tf_op jit(solution)/shard_map/ppermute | solution.py:544
  124.8 0.3 collective-permute-start.38
  125.1 1.6 %backward_near.1 = (bf16[4,256,128]{2,1,0:T(8,128)(2,1)S(1)}, bf16[4,256,128]{2,1,0:T(8,128)(2,1)S(1)}) custom-call(s32[1,640]{1,0:T(1,128)S(1)} %get-tuple-element.150.list_ref, s32[1,384]{1,0:T(1,128)S(1)} %get-tuple-element.118.tgt_ref, bf16[384,128,128]{2,1,0:T(8,128)(2,1)S(1)} %get-tuple-element.89.held, f32[32,256,128]{2,1,0:T(8,128)S(1)} %backward_early.1.early, ...), custom_call_target="tpu_custom_call" | custom-call | flops 1610612736 | bytes 12582912 | tf_op jit(solution)/shard_map/backward_near/pallas_call | solution.py:257
  126.7 2.4 %collective-permute-done.38 = bf16[136,256]{1,0:T(8,128)(2,1)S(1)} collective-permute-done((bf16[136,256]{1,0:T(8,128)(2,1)S(1)}, bf16[136,256]{1,0:T(8,128)(2,1)S(1)}, u32[]{:S(2)}, u32[]{:S(2)}) %collective-permute-start.38) | collective-permute-done | bytes 69664 | tf_op jit(solution)/shard_map/ppermute | solution.py:619
  129.2 3.0 %collective-permute-done.36 = bf16[6,256,128]{2,1,0:T(8,128)(2,1)S(1)} collective-permute-done((bf16[6,256,128]{2,1,0:T(8,128)(2,1)S(1)}, bf16[6,256,128]{2,1,0:T(8,128)(2,1)S(1)}, u32[]{:S(2)}, u32[]{:S(2)}) %collective-permute-start.36) | collective-permute-done | bytes 393248 | tf_op jit(solution)/shard_map/ppermute | solution.py:544
  132.4 1.2 collective-permute-start.39
  133.8 3.2 %collective-permute-start.41 = (bf16[4,256,128]{2,1,0:T(8,128)(2,1)S(1)}, bf16[4,256,128]{2,1,0:T(8,128)(2,1)S(1)}, u32[]{:S(2)}, u32[]{:S(2)}) collective-permute-start(bf16[4,256,128]{2,1,0:T(8,128)(2,1)S(1)} %get-tuple-element.161), channel_id=1, source_target_pairs={{16,0},{32,16},{48,32},{0,48},{80,64},{96,80},{112,96},{64,112},{1... | collective-permute-start | bytes 786440 | tf_op jit(solution)/shard_map/ppermute | solution.py:544
  137.0 2.5 %collective-permute-start.43 = (bf16[136,256]{1,0:T(8,128)(2,1)S(1)}, bf16[136,256]{1,0:T(8,128)(2,1)S(1)}, u32[]{:S(2)}, u32[]{:S(2)}) collective-permute-start(bf16[136,256]{1,0:T(8,128)(2,1)S(1)} %add_convert_fusion.2.refs_0_), channel_id=1, source_target_pairs={{4,0},{5,1},{6,2},{7,3},{0,4},{1,5},{2,6},{3,7},{12,8},{13,9},{14,... | collective-permute-start | bytes 208904 | tf_op jit(solution)/shard_map/ppermute | solution.py:619
  139.5 0.2 collective-permute-start.44
  139.7 0.6 collective-permute-done.39.across
  140.4 2.4 %collective-permute-done.43.refs_1_ = bf16[136,256]{1,0:T(8,128)(2,1)S(1)} collective-permute-done((bf16[136,256]{1,0:T(8,128)(2,1)S(1)}, bf16[136,256]{1,0:T(8,128)(2,1)S(1)}, u32[]{:S(2)}, u32[]{:S(2)}) %collective-permute-start.43) | collective-permute-done | bytes 69664 | tf_op jit(solution)/shard_map/ppermute | solution.py:619
  142.8 2.4 %collective-permute-done.44.refs_3_ = bf16[136,256]{1,0:T(8,128)(2,1)S(1)} collective-permute-done((bf16[136,256]{1,0:T(8,128)(2,1)S(1)}, bf16[136,256]{1,0:T(8,128)(2,1)S(1)}, u32[]{:S(2)}, u32[]{:S(2)}) %collective-permute-start.44) | collective-permute-done | bytes 69664 | tf_op jit(solution)/shard_map/ppermute | solution.py:619
  145.2 1.5 %finish_grads.1 = (bf16[512,256]{1,0:T(8,128)(2,1)}, f32[256,256]{1,0:T(8,128)}, f32[1,256]{1,0:T(1,128)}) custom-call(f32[4,256,128]{2,1,0:T(8,128)S(1)} %add_across.1.here, bf16[4,256,128]{2,1,0:T(8,128)(2,1)S(1)} %collective-permute-done.40.up, bf16[4,256,128]{2,1,0:T(8,128)(2,1)S(1)} %collective-permute-done.41.down, s32[8]{0:T(128)S(1)} %copy-done.3, ...), custom_call_target="tpu_custom_call" | custom-call | tf_op jit(solution)/shard_map/finish_grads/pallas_call | solution.py:475
  (81 shorter events, 2.7 us)
Async XLA Ops:
  0.6 12.7 %collective-permute-start = (bf16[4,128,256]{2,1,0:T(8,128)(2,1)}, bf16[4,128,256]{2,1,0:T(8,128)(2,1)S(1)}, u32[]{:S(2)}, u32[]{:S(2)}) collective-permute-start(bf16[4,128,256]{2,1,0:T(8,128)(2,1)} %bitcast.21), channel_id=1, source_target_pairs={{64,0},{80,16},{96,32},{112,48},{0,64},{16,80},{32,96},{48,112},{6... | collective-permute-start | bytes 786440 | tf_op jit(solution)/shard_map/ppermute | solution.py:544
  4.0 9.6 %collective-permute-start.1 = (bf16[4,128,256]{2,1,0:T(8,128)(2,1)}, bf16[4,128,256]{2,1,0:T(8,128)(2,1)S(1)}, u32[]{:S(2)}, u32[]{:S(2)}) collective-permute-start(bf16[4,128,256]{2,1,0:T(8,128)(2,1)} %bitcast.22), channel_id=1, source_target_pairs={{16,0},{32,16},{48,32},{0,48},{80,64},{96,80},{112,96},{64,112},{1... | collective-permute-start | bytes 786440 | tf_op jit(solution)/shard_map/ppermute | solution.py:544
  8.0 8.9 %collective-permute-start.2 = (bf16[4,128,256]{2,1,0:T(8,128)(2,1)}, bf16[4,128,256]{2,1,0:T(8,128)(2,1)S(1)}, u32[]{:S(2)}, u32[]{:S(2)}) collective-permute-start(bf16[4,128,256]{2,1,0:T(8,128)(2,1)} %bitcast.23), channel_id=1, source_target_pairs={{48,0},{0,16},{16,32},{32,48},{112,64},{64,80},{80,96},{96,112},{4... | collective-permute-start | bytes 786440 | tf_op jit(solution)/shard_map/ppermute | solution.py:544
  9.4 12.0 %copy-start = (bf16[512,256]{1,0:T(8,128)(2,1)S(1)}, bf16[512,256]{1,0:T(8,128)(2,1)}, u32[]{:S(2)}) copy-start(bf16[512,256]{1,0:T(8,128)(2,1)} %param.8) | copy-start | bytes 786436
  16.9 8.5 %collective-permute-start.3 = (bf16[4,128,256]{2,1,0:T(8,128)(2,1)S(1)}, bf16[4,128,256]{2,1,0:T(8,128)(2,1)S(1)}, u32[]{:S(2)}, u32[]{:S(2)}) collective-permute-start(bf16[4,128,256]{2,1,0:T(8,128)(2,1)S(1)} %collective-permute-done.refs_2_), channel_id=1, source_target_pairs={{16,0},{32,16},{48,32},{0,48},{80,64},{96,80},{112,96},{64,112},{1... | collective-permute-start | bytes 786440 | tf_op jit(solution)/shard_map/ppermute | solution.py:544
  17.9 8.7 %collective-permute-start.4 = (bf16[4,128,256]{2,1,0:T(8,128)(2,1)S(1)}, bf16[4,128,256]{2,1,0:T(8,128)(2,1)S(1)}, u32[]{:S(2)}, u32[]{:S(2)}) collective-permute-start(bf16[4,128,256]{2,1,0:T(8,128)(2,1)S(1)} %collective-permute-done.refs_2_), channel_id=1, source_target_pairs={{48,0},{0,16},{16,32},{32,48},{112,64},{64,80},{80,96},{96,112},{4... | collective-permute-start | bytes 786440 | tf_op jit(solution)/shard_map/ppermute | solution.py:544
  19.0 10.9 %collective-permute-start.5 = (bf16[2,128,256]{2,1,0:T(8,128)(2,1)S(1)}, bf16[2,128,256]{2,1,0:T(8,128)(2,1)S(1)}, u32[]{:S(2)}, u32[]{:S(2)}) collective-permute-start(bf16[2,128,256]{2,1,0:T(8,128)(2,1)S(1)} %slice.45), channel_id=1, source_target_pairs={{16,0},{32,16},{48,32},{0,48},{80,64},{96,80},{112,96},{64,112},{1... | collective-permute-start | bytes 393224 | tf_op jit(solution)/shard_map/ppermute | solution.py:544
  21.2 8.6 %collective-permute-start.6 = (bf16[2,128,256]{2,1,0:T(8,128)(2,1)S(1)}, bf16[2,128,256]{2,1,0:T(8,128)(2,1)S(1)}, u32[]{:S(2)}, u32[]{:S(2)}) collective-permute-start(bf16[2,128,256]{2,1,0:T(8,128)(2,1)S(1)} %slice.46), channel_id=1, source_target_pairs={{48,0},{0,16},{16,32},{32,48},{112,64},{64,80},{80,96},{96,112},{4... | collective-permute-start | bytes 393224 | tf_op jit(solution)/shard_map/ppermute | solution.py:544
  26.6 5.7 %collective-permute-start.7 = (bf16[2,128,256]{2,1,0:T(8,128)(2,1)S(1)}, bf16[2,128,256]{2,1,0:T(8,128)(2,1)S(1)}, u32[]{:S(2)}, u32[]{:S(2)}) collective-permute-start(bf16[2,128,256]{2,1,0:T(8,128)(2,1)S(1)} %slice.47), channel_id=1, source_target_pairs={{16,0},{32,16},{48,32},{0,48},{80,64},{96,80},{112,96},{64,112},{1... | collective-permute-start | bytes 393224 | tf_op jit(solution)/shard_map/ppermute | solution.py:544
  29.7 6.2 %collective-permute-start.8 = (bf16[2,128,256]{2,1,0:T(8,128)(2,1)S(1)}, bf16[2,128,256]{2,1,0:T(8,128)(2,1)S(1)}, u32[]{:S(2)}, u32[]{:S(2)}) collective-permute-start(bf16[2,128,256]{2,1,0:T(8,128)(2,1)S(1)} %slice.48), channel_id=1, source_target_pairs={{48,0},{0,16},{16,32},{32,48},{112,64},{64,80},{80,96},{96,112},{4... | collective-permute-start | bytes 393224 | tf_op jit(solution)/shard_map/ppermute | solution.py:544
  39.7 14.1 %collective-permute-start.10 = (bf16[2,3,4,128,256]{4,3,2,1,0:T(8,128)(2,1)S(1)}, bf16[2,3,4,128,256]{4,3,2,1,0:T(8,128)(2,1)S(1)}, u32[]{:S(2)}, u32[]{:S(2)}) collective-permute-start(bf16[2,3,4,128,256]{4,3,2,1,0:T(8,128)(2,1)S(1)} %get-tuple-element.99), channel_id=1, source_target_pairs={{1,0},{0,1},{3,2},{2,3},{5,4},{4,5},{7,6},{6,7},{9,8},{8,9},{11,10... | collective-permute-start | bytes 4718600 | tf_op jit(solution)/shard_map/ppermute | solution.py:552
  39.8 4.1 %collective-permute-start.9 = (bf16[2,4,128,256]{3,2,1,0:T(8,128)(2,1)S(1)}, bf16[2,4,128,256]{3,2,1,0:T(8,128)(2,1)S(1)}, u32[]{:S(2)}, u32[]{:S(2)}) collective-permute-start(bf16[2,4,128,256]{3,2,1,0:T(8,128)(2,1)S(1)} %get-tuple-element.97), channel_id=1, source_target_pairs={{1,0},{0,1},{3,2},{2,3},{5,4},{4,5},{7,6},{6,7},{9,8},{8,9},{11,10... | collective-permute-start | bytes 1572872 | tf_op jit(solution)/shard_map/ppermute | solution.py:552
  44.1 9.6 %collective-permute-start.11 = (bf16[2,2,128,256]{3,2,1,0:T(8,128)(2,1)S(1)}, bf16[2,2,128,256]{3,2,1,0:T(8,128)(2,1)S(1)}, u32[]{:S(2)}, u32[]{:S(2)}) collective-permute-start(bf16[2,2,128,256]{3,2,1,0:T(8,128)(2,1)S(1)} %get-tuple-element.100), channel_id=1, source_target_pairs={{6,0},{7,1},{0,2},{1,3},{2,4},{3,5},{4,6},{5,7},{14,8},{15,9},{8,1... | collective-permute-start | bytes 786440 | tf_op jit(solution)/shard_map/ppermute | solution.py:552
  44.2 9.5 %collective-permute-start.12 = (bf16[2,2,128,256]{3,2,1,0:T(8,128)(2,1)S(1)}, bf16[2,2,128,256]{3,2,1,0:T(8,128)(2,1)S(1)}, u32[]{:S(2)}, u32[]{:S(2)}) collective-permute-start(bf16[2,2,128,256]{3,2,1,0:T(8,128)(2,1)S(1)} %get-tuple-element.101), channel_id=1, source_target_pairs={{2,0},{3,1},{4,2},{5,3},{6,4},{7,5},{0,6},{1,7},{10,8},{11,9},{12,... | collective-permute-start | bytes 786440 | tf_op jit(solution)/shard_map/ppermute | solution.py:552
  49.6 7.9 %copy-start.3 = (s32[8]{0:T(128)S(1)}, s32[8]{0:T(128)}, u32[]{:S(2)}) copy-start(s32[8]{0:T(128)} %stack.31.meta.refs_4_) | copy-start | bytes 100
  49.6 7.9 %copy-start.4 = (s32[1,384]{1,0:T(1,128)S(1)}, s32[1,384]{1,0:T(1,128)}, u32[]{:S(2)}) copy-start(s32[1,384]{1,0:T(1,128)} %rows.3) | copy-start | bytes 4612
  49.6 7.9 %copy-start.5 = (s32[1,384]{1,0:T(1,128)S(1)}, s32[1,384]{1,0:T(1,128)}, u32[]{:S(2)}) copy-start(s32[1,384]{1,0:T(1,128)} %cols.3) | copy-start | bytes 4612
  49.6 23.2 %copy-start.1 = (bf16[512,256]{1,0:T(8,128)(2,1)S(1)}, bf16[512,256]{1,0:T(8,128)(2,1)}, u32[]{:S(2)}) copy-start(bf16[512,256]{1,0:T(8,128)(2,1)} %refs_7_.1) | copy-start | bytes 786436
  49.6 23.1 %copy-start.2 = (bf16[256,256]{1,0:T(8,128)(2,1)S(1)}, bf16[256,256]{1,0:T(8,128)(2,1)}, u32[]{:S(2)}) copy-start(bf16[256,256]{1,0:T(8,128)(2,1)} %refs_5_.1) | copy-start | bytes 393220
  49.6 23.1 %copy-start.6 = (f32[256]{0:T(256)S(1)}, f32[256]{0:T(256)}, u32[]{:S(2)}) copy-start(f32[256]{0:T(256)} %param.10) | copy-start | bytes 3076
  54.2 8.8 %collective-permute-start.13 = (bf16[4,128,256]{2,1,0:T(8,128)(2,1)S(1)}, bf16[4,128,256]{2,1,0:T(8,128)(2,1)S(1)}, u32[]{:S(2)}, u32[]{:S(2)}) collective-permute-start(bf16[4,128,256]{2,1,0:T(8,128)(2,1)S(1)} %get-tuple-element.105), channel_id=1, source_target_pairs={{6,0},{7,1},{0,2},{1,3},{2,4},{3,5},{4,6},{5,7},{14,8},{15,9},{8,1... | collective-permute-start | bytes 786440 | tf_op jit(solution)/shard_map/ppermute | solution.py:552
  54.3 8.7 %collective-permute-start.14 = (bf16[4,128,256]{2,1,0:T(8,128)(2,1)S(1)}, bf16[4,128,256]{2,1,0:T(8,128)(2,1)S(1)}, u32[]{:S(2)}, u32[]{:S(2)}) collective-permute-start(bf16[4,128,256]{2,1,0:T(8,128)(2,1)S(1)} %get-tuple-element.106), channel_id=1, source_target_pairs={{2,0},{3,1},{4,2},{5,3},{6,4},{7,5},{0,6},{1,7},{10,8},{11,9},{12,... | collective-permute-start | bytes 786440 | tf_op jit(solution)/shard_map/ppermute | solution.py:552
  63.1 7.9 %collective-permute-start.15 = (bf16[4,128,256]{2,1,0:T(8,128)(2,1)S(1)}, bf16[4,128,256]{2,1,0:T(8,128)(2,1)S(1)}, u32[]{:S(2)}, u32[]{:S(2)}) collective-permute-start(bf16[4,128,256]{2,1,0:T(8,128)(2,1)S(1)} %get-tuple-element.108), channel_id=1, source_target_pairs={{6,0},{7,1},{0,2},{1,3},{2,4},{3,5},{4,6},{5,7},{14,8},{15,9},{8,1... | collective-permute-start | bytes 786440 | tf_op jit(solution)/shard_map/ppermute | solution.py:552
  64.0 7.0 %collective-permute-start.16 = (bf16[4,128,256]{2,1,0:T(8,128)(2,1)S(1)}, bf16[4,128,256]{2,1,0:T(8,128)(2,1)S(1)}, u32[]{:S(2)}, u32[]{:S(2)}) collective-permute-start(bf16[4,128,256]{2,1,0:T(8,128)(2,1)S(1)} %get-tuple-element.109), channel_id=1, source_target_pairs={{2,0},{3,1},{4,2},{5,3},{6,4},{7,5},{0,6},{1,7},{10,8},{11,9},{12,... | collective-permute-start | bytes 786440 | tf_op jit(solution)/shard_map/ppermute | solution.py:552
  66.4 6.4 %collective-permute-start.17 = (bf16[4,128,256]{2,1,0:T(8,128)(2,1)S(1)}, bf16[4,128,256]{2,1,0:T(8,128)(2,1)S(1)}, u32[]{:S(2)}, u32[]{:S(2)}) collective-permute-start(bf16[4,128,256]{2,1,0:T(8,128)(2,1)S(1)} %fusion.1), channel_id=1, source_target_pairs={{8,0},{9,1},{10,2},{11,3},{12,4},{13,5},{14,6},{15,7},{0,8},{1,9},... | collective-permute-start | bytes 786440 | tf_op jit(solution)/shard_map/ppermute | solution.py:552
  74.8 6.4 %collective-permute-start.18 = (bf16[4,256,128]{2,1,0:T(8,128)(2,1)S(1)}, bf16[4,256,128]{2,1,0:T(8,128)(2,1)S(1)}, u32[]{:S(2)}, u32[]{:S(2)}) collective-permute-start(bf16[4,256,128]{2,1,0:T(8,128)(2,1)S(1)} %get-tuple-element.113.refs_0_), channel_id=1, source_target_pairs={{8,0},{9,1},{10,2},{11,3},{12,4},{13,5},{14,6},{15,7},{0,8},{1,9},... | collective-permute-start | bytes 786440 | tf_op jit(solution)/shard_map/ppermute | solution.py:552
  74.8 6.4 %collective-permute-start.20 = (bf16[4,256,128]{2,1,0:T(8,128)(2,1)S(1)}, bf16[4,256,128]{2,1,0:T(8,128)(2,1)S(1)}, u32[]{:S(2)}, u32[]{:S(2)}) collective-permute-start(bf16[4,256,128]{2,1,0:T(8,128)(2,1)S(1)} %get-tuple-element.113.refs_0_), channel_id=1, source_target_pairs={{2,0},{3,1},{4,2},{5,3},{6,4},{7,5},{0,6},{1,7},{10,8},{11,9},{12,... | collective-permute-start | bytes 786440 | tf_op jit(solution)/shard_map/ppermute | solution.py:552
  76.6 7.6 %collective-permute-start.22 = (bf16[4,256,128]{2,1,0:T(8,128)(2,1)S(1)}, bf16[4,256,128]{2,1,0:T(8,128)(2,1)S(1)}, u32[]{:S(2)}, u32[]{:S(2)}) collective-permute-start(bf16[4,256,128]{2,1,0:T(8,128)(2,1)S(1)} %get-tuple-element.113.refs_0_), channel_id=1, source_target_pairs={{6,0},{7,1},{0,2},{1,3},{2,4},{3,5},{4,6},{5,7},{14,8},{15,9},{8,1... | collective-permute-start | bytes 786440 | tf_op jit(solution)/shard_map/ppermute | solution.py:552
  76.8 1.4 collective-permute-start.19
  84.2 2.8 %collective-permute-start.26 = (bf16[12,256,128]{2,1,0:T(8,128)(2,1)S(1)}, bf16[12,256,128]{2,1,0:T(8,128)(2,1)S(1)}, u32[]{:S(2)}, u32[]{:S(2)}) collective-permute-start(bf16[12,256,128]{2,1,0:T(8,128)(2,1)S(1)} %pad_maximum_fusion), channel_id=1, source_target_pairs={{1,0},{0,1},{3,2},{2,3},{5,4},{4,5},{7,6},{6,7},{9,8},{8,9},{11,10... | collective-permute-start | bytes 2359304 | tf_op jit(solution)/shard_map/ppermute | solution.py:552
  84.3 2.7 %collective-permute-start.25 = (bf16[4,256,128]{2,1,0:T(8,128)(2,1)S(1)}, bf16[4,256,128]{2,1,0:T(8,128)(2,1)S(1)}, u32[]{:S(2)}, u32[]{:S(2)}) collective-permute-start(bf16[4,256,128]{2,1,0:T(8,128)(2,1)S(1)} %get-tuple-element.113.refs_0_), channel_id=1, source_target_pairs={{1,0},{0,1},{3,2},{2,3},{5,4},{4,5},{7,6},{6,7},{9,8},{8,9},{11,10... | collective-permute-start | bytes 786440 | tf_op jit(solution)/shard_map/ppermute | solution.py:552
  84.9 11.2 %collective-permute-start.21 = (bf16[6,256,128]{2,1,0:T(8,128)(2,1)S(1)}, bf16[6,256,128]{2,1,0:T(8,128)(2,1)S(1)}, u32[]{:S(2)}, u32[]{:S(2)}) collective-permute-start(bf16[6,256,128]{2,1,0:T(8,128)(2,1)S(1)} %get-tuple-element.171), channel_id=1, source_target_pairs={{2,0},{3,1},{4,2},{5,3},{6,4},{7,5},{0,6},{1,7},{10,8},{11,9},{12,... | collective-permute-start | bytes 1179656 | tf_op jit(solution)/shard_map/ppermute | solution.py:552
  85.0 12.4 %collective-permute-start.23 = (bf16[6,256,128]{2,1,0:T(8,128)(2,1)S(1)}, bf16[6,256,128]{2,1,0:T(8,128)(2,1)S(1)}, u32[]{:S(2)}, u32[]{:S(2)}) collective-permute-start(bf16[6,256,128]{2,1,0:T(8,128)(2,1)S(1)} %get-tuple-element.170), channel_id=1, source_target_pairs={{6,0},{7,1},{0,2},{1,3},{2,4},{3,5},{4,6},{5,7},{14,8},{15,9},{8,1... | collective-permute-start | bytes 1179656 | tf_op jit(solution)/shard_map/ppermute | solution.py:552
  87.0 5.1 %collective-permute-start.24 = (f32[136,256]{1,0:T(8,128)S(1)}, f32[136,256]{1,0:T(8,128)S(1)}, u32[]{:S(2)}, u32[]{:S(2)}) collective-permute-start(f32[136,256]{1,0:T(8,128)S(1)} %add.36), channel_id=1, source_target_pairs={{16,0},{0,16},{48,32},{32,48},{80,64},{64,80},{112,96},{96,112},{1... | collective-permute-start | bytes 417800 | tf_op jit(solution)/shard_map/ppermute | solution.py:619
  97.5 10.8 %collective-permute-start.30 = (bf16[12,256,128]{2,1,0:T(8,128)(2,1)S(1)}, bf16[12,256,128]{2,1,0:T(8,128)(2,1)S(1)}, u32[]{:S(2)}, u32[]{:S(2)}) collective-permute-start(bf16[12,256,128]{2,1,0:T(8,128)(2,1)S(1)} %pad_maximum_fusion.1), channel_id=1, source_target_pairs={{1,0},{0,1},{3,2},{2,3},{5,4},{4,5},{7,6},{6,7},{9,8},{8,9},{11,10... | collective-permute-start | bytes 2359304 | tf_op jit(solution)/shard_map/ppermute | solution.py:552
  97.6 9.1 %collective-permute-start.29 = (f32[136,256]{1,0:T(8,128)S(1)}, f32[136,256]{1,0:T(8,128)S(1)}, u32[]{:S(2)}, u32[]{:S(2)}) collective-permute-start(f32[136,256]{1,0:T(8,128)S(1)} %add.37), channel_id=1, source_target_pairs={{8,0},{9,1},{10,2},{11,3},{12,4},{13,5},{14,6},{15,7},{0,8},{1,9},... | collective-permute-start | bytes 417800 | tf_op jit(solution)/shard_map/ppermute | solution.py:619
  99.7 5.6 %collective-permute-start.27 = (bf16[2,256,128]{2,1,0:T(8,128)(2,1)S(1)}, bf16[2,256,128]{2,1,0:T(8,128)(2,1)S(1)}, u32[]{:S(2)}, u32[]{:S(2)}) collective-permute-start(bf16[2,256,128]{2,1,0:T(8,128)(2,1)S(1)} %slice.54), channel_id=1, source_target_pairs={{2,0},{3,1},{4,2},{5,3},{6,4},{7,5},{0,6},{1,7},{10,8},{11,9},{12,... | collective-permute-start | bytes 393224 | tf_op jit(solution)/shard_map/ppermute | solution.py:552
  100.0 6.6 %collective-permute-start.28 = (bf16[2,256,128]{2,1,0:T(8,128)(2,1)S(1)}, bf16[2,256,128]{2,1,0:T(8,128)(2,1)S(1)}, u32[]{:S(2)}, u32[]{:S(2)}) collective-permute-start(bf16[2,256,128]{2,1,0:T(8,128)(2,1)S(1)} %slice.55), channel_id=1, source_target_pairs={{6,0},{7,1},{0,2},{1,3},{2,4},{3,5},{4,6},{5,7},{14,8},{15,9},{8,1... | collective-permute-start | bytes 393224 | tf_op jit(solution)/shard_map/ppermute | solution.py:552
  106.7 1.6 %collective-permute-start.31 = (bf16[4,256,128]{2,1,0:T(8,128)(2,1)S(1)}, bf16[4,256,128]{2,1,0:T(8,128)(2,1)S(1)}, u32[]{:S(2)}, u32[]{:S(2)}) collective-permute-start(bf16[4,256,128]{2,1,0:T(8,128)(2,1)S(1)} %pad_maximum_fusion.4), channel_id=1, source_target_pairs={{1,0},{0,1},{3,2},{2,3},{5,4},{4,5},{7,6},{6,7},{9,8},{8,9},{11,10... | collective-permute-start | bytes 786440 | tf_op jit(solution)/shard_map/ppermute | solution.py:552
  106.8 8.8 %collective-permute-start.32 = (bf16[136,256]{1,0:T(8,128)(2,1)S(1)}, bf16[136,256]{1,0:T(8,128)(2,1)S(1)}, u32[]{:S(2)}, u32[]{:S(2)}) collective-permute-start(bf16[136,256]{1,0:T(8,128)(2,1)S(1)} %add.38), channel_id=1, source_target_pairs={{32,0},{48,16},{0,32},{16,48},{96,64},{112,80},{64,96},{80,112},{3... | collective-permute-start | bytes 208904 | tf_op jit(solution)/shard_map/ppermute | solution.py:619
  112.3 6.8 %collective-permute-start.34 = (bf16[2,256,128]{2,1,0:T(8,128)(2,1)S(1)}, bf16[2,256,128]{2,1,0:T(8,128)(2,1)S(1)}, u32[]{:S(2)}, u32[]{:S(2)}) collective-permute-start(bf16[2,256,128]{2,1,0:T(8,128)(2,1)S(1)} %get-tuple-element.141), channel_id=1, source_target_pairs={{48,0},{0,16},{16,32},{32,48},{112,64},{64,80},{80,96},{96,112},{4... | collective-permute-start | bytes 393224 | tf_op jit(solution)/shard_map/ppermute | solution.py:544
  112.4 6.7 %collective-permute-start.35 = (bf16[2,256,128]{2,1,0:T(8,128)(2,1)S(1)}, bf16[2,256,128]{2,1,0:T(8,128)(2,1)S(1)}, u32[]{:S(2)}, u32[]{:S(2)}) collective-permute-start(bf16[2,256,128]{2,1,0:T(8,128)(2,1)S(1)} %get-tuple-element.142), channel_id=1, source_target_pairs={{16,0},{32,16},{48,32},{0,48},{80,64},{96,80},{112,96},{64,112},{1... | collective-permute-start | bytes 393224 | tf_op jit(solution)/shard_map/ppermute | solution.py:544
  115.6 5.9 %collective-permute-start.33 = (bf16[136,256]{1,0:T(8,128)(2,1)S(1)}, bf16[136,256]{1,0:T(8,128)(2,1)S(1)}, u32[]{:S(2)}, u32[]{:S(2)}) collective-permute-start(bf16[136,256]{1,0:T(8,128)(2,1)S(1)} %add_convert_fusion.3), channel_id=1, source_target_pairs={{64,0},{80,16},{96,32},{112,48},{0,64},{16,80},{32,96},{48,112},{6... | collective-permute-start | bytes 208904 | tf_op jit(solution)/shard_map/ppermute | solution.py:619
  121.5 10.7 %collective-permute-start.36 = (bf16[6,256,128]{2,1,0:T(8,128)(2,1)S(1)}, bf16[6,256,128]{2,1,0:T(8,128)(2,1)S(1)}, u32[]{:S(2)}, u32[]{:S(2)}) collective-permute-start(bf16[6,256,128]{2,1,0:T(8,128)(2,1)S(1)} %get-tuple-element.147), channel_id=1, source_target_pairs={{48,0},{0,16},{16,32},{32,48},{112,64},{64,80},{80,96},{96,112},{4... | collective-permute-start | bytes 1179656 | tf_op jit(solution)/shard_map/ppermute | solution.py:544
  121.5 10.7 %collective-permute-start.37 = (bf16[6,256,128]{2,1,0:T(8,128)(2,1)S(1)}, bf16[6,256,128]{2,1,0:T(8,128)(2,1)S(1)}, u32[]{:S(2)}, u32[]{:S(2)}) collective-permute-start(bf16[6,256,128]{2,1,0:T(8,128)(2,1)S(1)} %get-tuple-element.148), channel_id=1, source_target_pairs={{16,0},{32,16},{48,32},{0,48},{80,64},{96,80},{112,96},{64,112},{1... | collective-permute-start | bytes 1179656 | tf_op jit(solution)/shard_map/ppermute | solution.py:544
  124.8 4.4 %collective-permute-start.38 = (bf16[136,256]{1,0:T(8,128)(2,1)S(1)}, bf16[136,256]{1,0:T(8,128)(2,1)S(1)}, u32[]{:S(2)}, u32[]{:S(2)}) collective-permute-start(bf16[136,256]{1,0:T(8,128)(2,1)S(1)} %convert_add_fusion), channel_id=1, source_target_pairs={{2,0},{3,1},{0,2},{1,3},{6,4},{7,5},{4,6},{5,7},{10,8},{11,9},{8,1... | collective-permute-start | bytes 208904 | tf_op jit(solution)/shard_map/ppermute | solution.py:619
  132.4 8.0 %collective-permute-start.39 = (bf16[4,256,128]{2,1,0:T(8,128)(2,1)S(1)}, bf16[4,256,128]{2,1,0:T(8,128)(2,1)S(1)}, u32[]{:S(2)}, u32[]{:S(2)}) collective-permute-start(bf16[4,256,128]{2,1,0:T(8,128)(2,1)S(1)} %add_convert_fusion.1), channel_id=1, source_target_pairs={{64,0},{80,16},{96,32},{112,48},{0,64},{16,80},{32,96},{48,112},{6... | collective-permute-start | bytes 786440 | tf_op jit(solution)/shard_map/ppermute | solution.py:544
  133.6 3.4 %collective-permute-start.42 = (bf16[136,256]{1,0:T(8,128)(2,1)S(1)}, bf16[136,256]{1,0:T(8,128)(2,1)S(1)}, u32[]{:S(2)}, u32[]{:S(2)}) collective-permute-start(bf16[136,256]{1,0:T(8,128)(2,1)S(1)} %add_convert_fusion.2.refs_0_), channel_id=1, source_target_pairs={{1,0},{0,1},{3,2},{2,3},{5,4},{4,5},{7,6},{6,7},{9,8},{8,9},{11,10... | collective-permute-start | bytes 208904 | tf_op jit(solution)/shard_map/ppermute | solution.py:552
  133.7 11.6 %collective-permute-start.40 = (bf16[4,256,128]{2,1,0:T(8,128)(2,1)S(1)}, bf16[4,256,128]{2,1,0:T(8,128)(2,1)S(1)}, u32[]{:S(2)}, u32[]{:S(2)}) collective-permute-start(bf16[4,256,128]{2,1,0:T(8,128)(2,1)S(1)} %get-tuple-element.160), channel_id=1, source_target_pairs={{48,0},{0,16},{16,32},{32,48},{112,64},{64,80},{80,96},{96,112},{4... | collective-permute-start | bytes 786440 | tf_op jit(solution)/shard_map/ppermute | solution.py:544
  133.8 11.5 %collective-permute-start.41 = (bf16[4,256,128]{2,1,0:T(8,128)(2,1)S(1)}, bf16[4,256,128]{2,1,0:T(8,128)(2,1)S(1)}, u32[]{:S(2)}, u32[]{:S(2)}) collective-permute-start(bf16[4,256,128]{2,1,0:T(8,128)(2,1)S(1)} %get-tuple-element.161), channel_id=1, source_target_pairs={{16,0},{32,16},{48,32},{0,48},{80,64},{96,80},{112,96},{64,112},{1... | collective-permute-start | bytes 786440 | tf_op jit(solution)/shard_map/ppermute | solution.py:544
  137.0 5.8 %collective-permute-start.43 = (bf16[136,256]{1,0:T(8,128)(2,1)S(1)}, bf16[136,256]{1,0:T(8,128)(2,1)S(1)}, u32[]{:S(2)}, u32[]{:S(2)}) collective-permute-start(bf16[136,256]{1,0:T(8,128)(2,1)S(1)} %add_convert_fusion.2.refs_0_), channel_id=1, source_target_pairs={{4,0},{5,1},{6,2},{7,3},{0,4},{1,5},{2,6},{3,7},{12,8},{13,9},{14,... | collective-permute-start | bytes 208904 | tf_op jit(solution)/shard_map/ppermute | solution.py:619
  139.5 5.8 %collective-permute-start.44 = (bf16[136,256]{1,0:T(8,128)(2,1)S(1)}, bf16[136,256]{1,0:T(8,128)(2,1)S(1)}, u32[]{:S(2)}, u32[]{:S(2)}) collective-permute-start(bf16[136,256]{1,0:T(8,128)(2,1)S(1)} %add_convert_fusion.2.refs_0_), channel_id=1, source_target_pairs={{5,0},{4,1},{7,2},{6,3},{1,4},{0,5},{3,6},{2,7},{13,8},{12,9},{15,... | collective-permute-start | bytes 208904 | tf_op jit(solution)/shard_map/ppermute | solution.py:619
